TPU v7x, 32 devices: a whole 2x2x4 slice. The times are simulated.
32 devices in a mesh: magnet: 4 (over y, x), slab: 8 (over z, core).
Axes of the slice: x: 2, y: 2, z: 4, core: 2. Of those that a mesh axis runs over, the one named last changes fastest.
Arguments:
- foil_warmth: float32 [256, 512], P(('magnet', 'slab')), may hold values from 0.5 to 4
- terminal_voltage_input: float32 [256, 512], P(('magnet', 'slab')), may hold values from -6 to 6
- foil_segment_pattern: int32 [256, 512], P(('magnet', 'slab')), may hold values from 0 to 2
- underlying_block_map: int32 [256, 512], P('magnet'), may hold values from 768 to 1023
- prior_block_warmth: float32 [8, 256, 128], P('slab', 'magnet'), may hold values from 0 to 2
- substance_kind: int32 [8, 256, 128], P('slab', 'magnet'), may hold values from 0 to 3
Outputs:
- sheet_potential: float32 [256, 512], P(('magnet', 'slab'))
- brick_heated: float32 [8, 256, 128], P('slab', 'magnet')
Inputs may be any that keep to these rules, and one draw needn't show every extreme that they name: `foil_segment_pattern`: 0 marks plain heater steel, 1 copper-plated stations, 2 current-lead contacts. `underlying_block_map`: the value is radial layer times 128 plus azimuthal cell. `substance_kind`: 0 insulation, 1 Nb3Sn coil, 2 copper wedge, 3 steel collar.
All inputs are finite; a program needn't handle non-finite values.
Results may differ from a plain program's by a relative error of at most 0.0001.
Values sent between devices are 32-bit elements; how exact they have to be, the bound alone decides.
A program may use at most 64 MiB of HBM per device.

v0:
```python
import jax
import jax.numpy as jnp
from jax import lax
from jax.sharding import PartitionSpec as P

ITERS = 3
SUBSTEPS = 4


leak_diag = 0.25
contact_gain = 4.0
copper_factor = 3.0
sheet_slope = 0.5
heat_factor = 1.5
time_step = 0.03
conduct_table = (0.3, 1.0, 2.0, 0.6)
capacity_table = (1.0, 1.5, 2.0, 1.2)
diffusivity_derivative = 0.4


def padded_2(shard, sides, width):
    for axis, dim in sides:
        size, length = (lax.axis_size(axis), shard.shape[dim])
        up = [(i, (i + 1) % size) for i in range(size - 1)]
        down = [(j, i) for i, j in up]
        last = lax.slice_in_dim(shard, length - width, length, axis=dim)
        initial = lax.slice_in_dim(shard, 0, width, axis=dim)
        before = lax.ppermute(last, axis, up)
        after = lax.ppermute(initial, axis, down)
        shard = jnp.concatenate([before, shard, after], axis=dim)
    return shard


def lookup_table(substance_kind, table):
    running_total = jnp.zeros(substance_kind.shape, jnp.float32)
    for material_index in range(4):
        running_total = running_total + jnp.where(
            substance_kind == material_index, table[material_index], 0.0
        ).astype(jnp.float32)
    return running_total


def sheet_padded(values_grid):
    extended_field = padded_2(values_grid, ((("magnet", "slab"), 0),), 1)
    return jnp.pad(extended_field, ((0, 0), (1, 1)))


def neighbour_values(padded):
    return (padded[:-2, 1:-1], padded[2:, 1:-1], padded[1:-1, :-2], padded[1:-1, 2:])


def apply_sheet(values_grid, coeffs, diagonal):
    neighbours = neighbour_values(sheet_padded(values_grid))
    result = diagonal * values_grid
    for coeff_face, neighbour in zip(coeffs, neighbours):
        result = result - coeff_face * neighbour
    return result


def squares_sum(residual):
    return lax.psum(jnp.sum(residual * residual), ("magnet", "slab"))


def diffusivity_update(temp_pad, cond_pad, resistive_power_density, specific_storage_grid):
    centre_t = temp_pad[1:-1, 1:-1]
    centre_k = cond_pad[1:-1, 1:-1]
    flux_total = jnp.zeros(centre_t.shape, jnp.float32)
    pairs = (
        (temp_pad[:-2, 1:-1], cond_pad[:-2, 1:-1]),
        (temp_pad[2:, 1:-1], cond_pad[2:, 1:-1]),
        (temp_pad[1:-1, :-2], cond_pad[1:-1, :-2]),
        (temp_pad[1:-1, 2:], cond_pad[1:-1, 2:]),
    )
    for other_t, other_k in pairs:
        flux_total = flux_total + 0.5 * (centre_k + other_k) * (other_t - centre_t)
    for offset in (1, -1):
        other_t = jnp.roll(centre_t, offset, axis=2)
        other_k = jnp.roll(centre_k, offset, axis=2)
        flux_total = flux_total + 0.5 * (centre_k + other_k) * (other_t - centre_t)
    return centre_t + time_step * (flux_total + resistive_power_density) / specific_storage_grid


def local(
    foil_warmth,
    terminal_voltage_input,
    foil_segment_pattern,
    underlying_block_map,
    prior_block_warmth,
    substance_kind,
):
    shells_per_device, axial_rows_per_device, angular_position = prior_block_warmth.shape
    copper = jnp.where(foil_segment_pattern == 1, copper_factor, 1.0).astype(jnp.float32)
    sigma_cells = copper / (1.0 + sheet_slope * foil_warmth)
    sigma_pad = sheet_padded(sigma_cells)
    centre = sigma_pad[1:-1, 1:-1]
    coeffs = tuple((0.5 * (centre + other) for other in neighbour_values(sigma_pad)))
    contact = jnp.where(foil_segment_pattern == 2, contact_gain, 0.0).astype(jnp.float32)
    diagonal = leak_diag + contact + coeffs[0] + coeffs[1] + coeffs[2] + coeffs[3]
    rhs_field = contact * terminal_voltage_input
    voltage_solution = jnp.zeros_like(rhs_field)
    residual = rhs_field
    direction = rhs_field
    norm_now = squares_sum(residual)
    for iteration in range(ITERS):
        image_field = apply_sheet(direction, coeffs, diagonal)
        curvature = lax.psum(jnp.sum(direction * image_field), ("magnet", "slab"))
        step_length = norm_now / curvature
        voltage_solution = voltage_solution + step_length * direction
        residual = residual - step_length * image_field
        if iteration + 1 < ITERS:
            norm_next = squares_sum(residual)
            direction = residual + norm_next / norm_now * direction
            norm_now = norm_next
    neighbours = neighbour_values(sheet_padded(voltage_solution))
    joule = jnp.zeros_like(voltage_solution)
    for coeff_face, neighbour in zip(coeffs, neighbours):
        joule = joule + coeff_face * (voltage_solution - neighbour) ** 2
    joule = heat_factor * joule
    slab_index = lax.axis_index("slab")
    reference_diffusivity = lookup_table(substance_kind, conduct_table)
    specific_storage_grid = lookup_table(substance_kind, capacity_table)
    gathered = lax.all_gather(joule, "slab", axis=0, tiled=True)
    block_cells = shells_per_device * angular_position
    local_cell = underlying_block_map - slab_index * block_cells
    inside = (local_cell >= 0) & (local_cell < block_cells)
    layer_index = jnp.where(inside, local_cell // angular_position, shells_per_device)
    column = local_cell % angular_position
    row_index = jnp.broadcast_to(
        jnp.arange(axial_rows_per_device, dtype=jnp.int32)[:, None], underlying_block_map.shape
    )
    resistive_power_density = (
        jnp.zeros((shells_per_device, axial_rows_per_device, angular_position), jnp.float32)
        .at[layer_index, row_index, column]
        .add(gathered, mode="drop")
    )
    warmth_distribution = prior_block_warmth
    for substep in range(SUBSTEPS):
        diffusivity_coefficient = reference_diffusivity * (
            1.0 + diffusivity_derivative * warmth_distribution
        )
        combined_shell_array = jnp.stack([warmth_distribution, diffusivity_coefficient])
        extended_field = padded_2(combined_shell_array, (("magnet", 2), ("slab", 1)), 1)
        warmth_distribution = diffusivity_update(
            extended_field[0], extended_field[1], resistive_power_density, specific_storage_grid
        )
    return (voltage_solution, warmth_distribution)


def solution(mesh):
    placed = (
        P(("magnet", "slab"), None),
        P(("magnet", "slab"), None),
        P(("magnet", "slab"), None),
        P("magnet", None),
        P("slab", "magnet", None),
        P("slab", "magnet", None),
    )
    return jax.shard_map(
        local,
        mesh=mesh,
        in_specs=placed,
        out_specs=(P(("magnet", "slab"), None), P("slab", "magnet", None)),
        check_vma=False,
    )
```

profile of v0, /device:TPU:9, one launch (start us, length us, event | category | flops | bytes accessed | tf_op | source)
XLA Modules:
  0.0 501.5 jit_solution(691510985378161167)
XLA Ops:
  1.5 2.7 collective-permute-start.3
  4.2 3.1 collective-permute-start.2
  9.2 3.6 collective-permute-start
  14.4 4.0 collective-permute-start.8
  19.4 46.4 %all-reduce.5 = (f32[]{:T(128)}, f32[]{:T(128)}) all-reduce(f32[]{:T(128)} %get-tuple-element.3, f32[]{:T(128)} %get-tuple-element.2), channel_id=1, replica_groups=mesh['magnet'=4,'slab'=8] {'magnet','slab'}, use_global_device_ids=true, to_apply=%region_1.2 | all-reduce | flops 2 | bytes 16 | tf_op jit(solution)/shard_map/psum | solution.py:61
  67.7 38.4 %psum.44 = f32[]{:T(128)} all-reduce(f32[]{:T(128)} %get-tuple-element.19), channel_id=1, replica_groups=mesh['magnet'=4,'slab'=8] {'magnet','slab'}, use_global_device_ids=true, to_apply=%region_5.6 | all-reduce | flops 1 | bytes 8 | tf_op jit(solution)/shard_map/psum | solution.py:61
  107.4 3.2 collective-permute-start.5
  110.6 2.9 collective-permute-start.4
  115.1 46.3 %psum.45 = f32[]{:T(128)} all-reduce(f32[]{:T(128)} %get-tuple-element.17), channel_id=1, replica_groups=mesh['magnet'=4,'slab'=8] {'magnet','slab'}, use_global_device_ids=true, to_apply=%region_7.8 | all-reduce | flops 1 | bytes 8 | tf_op jit(solution)/shard_map/psum | solution.py:106
  163.5 40.2 %psum.46 = f32[]{:T(128)} all-reduce(f32[]{:T(128)} %multiply_reduce_fusion.1), channel_id=1, replica_groups=mesh['magnet'=4,'slab'=8] {'magnet','slab'}, use_global_device_ids=true, to_apply=%region_9.10 | all-reduce | flops 1 | bytes 8 | tf_op jit(solution)/shard_map/psum | solution.py:61
  205.1 3.2 collective-permute-start.7
  212.6 44.4 %psum.47 = f32[]{:T(128)} all-reduce(f32[]{:T(128)} %fusion.112), channel_id=1, replica_groups=mesh['magnet'=4,'slab'=8] {'magnet','slab'}, use_global_device_ids=true, to_apply=%region_11.12 | all-reduce | flops 1 | bytes 8 | tf_op jit(solution)/shard_map/psum | solution.py:106
  258.4 3.1 collective-permute-start.13
  261.5 2.5 collective-permute-start.12
  265.9 3.6 collective-permute-start.10
  269.8 12.2 %all_gather.3 = f32[64,512]{1,0:T(8,128)S(1)} all-gather(f32[8,512]{1,0:T(8,128)S(1)} %fusion.99), channel_id=1, replica_groups=mesh['magnet'=4,'slab'=8] {'slab'}, dimensions={0}, use_global_device_ids=true | all-gather | bytes 147456 | tf_op jit(solution)/shard_map/all_gather | solution.py:122
  282.1 171.1 %scatter_custom_fusion = f32[8192]{0:T(1024)S(1)} fusion(s32[32768]{0:T(1024)S(1)} %bitcast.58, f32[32768]{0:T(1024)S(1)} %bitcast.59, f32[]{:T(128)} %constant.24.clone.1), kind=kCustom, calls=%fused_computation.254 | custom fusion | flops 32768 | bytes 32772
  454.8 5.9 %collective-permute-start.14 = (f32[2,1,1,128]{3,2,1,0:T(1,128)S(1)}, f32[2,1,1,128]{3,2,1,0:T(1,128)S(1)}, u32[]{:S(2)}, u32[]{:S(2)}) collective-permute-start(f32[2,1,1,128]{3,2,1,0:T(1,128)S(1)} %get-tuple-element.72), channel_id=1, source_target_pairs={{0,8},{8,16},{16,24},{1,9},{9,17},{17,25},{2,10},{10,18},{18,26},{... | collective-permute-start | bytes 3080 | tf_op jit(solution)/shard_map/ppermute | solution.py:28
  461.5 2.9 collective-permute-start.17
  464.4 2.6 collective-permute-start.16
  470.2 4.9 collective-permute-start.18
  475.8 4.7 collective-permute-start.21
  486.1 5.2 %collective-permute-start.22 = (f32[2,1,1,128]{3,2,1,0:T(1,128)S(1)}, f32[2,1,1,128]{3,2,1,0:T(1,128)S(1)}, u32[]{:S(2)}, u32[]{:S(2)}) collective-permute-start(f32[2,1,1,128]{3,2,1,0:T(1,128)S(1)} %get-tuple-element.68), channel_id=1, source_target_pairs={{0,8},{8,16},{16,24},{1,9},{9,17},{17,25},{2,10},{10,18},{18,26},{... | collective-permute-start | bytes 3080 | tf_op jit(solution)/shard_map/ppermute | solution.py:28
  492.0 5.0 collective-permute-start.25
  (109 shorter events, 31.4 us)
Async XLA Ops:
  1.5 13.0 %collective-permute-start.3 = (f32[1,512]{1,0:T(1,128)S(1)}, f32[1,512]{1,0:T(1,128)S(1)}, u32[]{:S(2)}, u32[]{:S(2)}) collective-permute-start(f32[1,512]{1,0:T(1,128)S(1)} %get-tuple-element.86), channel_id=1, source_target_pairs={{1,0},{2,1},{3,2},{4,3},{5,4},{6,5},{7,6},{8,7},{9,8},{10,9},{11,1... | collective-permute-start | bytes 6152 | tf_op jit(solution)/shard_map/ppermute | solution.py:29
  4.2 14.3 %collective-permute-start.2 = (f32[1,512]{1,0:T(1,128)S(1)}, f32[1,512]{1,0:T(1,128)S(1)}, u32[]{:S(2)}, u32[]{:S(2)}) collective-permute-start(f32[1,512]{1,0:T(1,128)S(1)} %get-tuple-element.85), channel_id=1, source_target_pairs={{0,1},{1,2},{2,3},{3,4},{4,5},{5,6},{6,7},{7,8},{8,9},{9,10},{10,1... | collective-permute-start | bytes 6152 | tf_op jit(solution)/shard_map/ppermute | solution.py:28
  7.3 11.2 %collective-permute-start.1 = (f32[1,512]{1,0:T(1,128)S(1)}, f32[1,512]{1,0:T(1,128)S(1)}, u32[]{:S(2)}, u32[]{:S(2)}) collective-permute-start(f32[1,512]{1,0:T(1,128)S(1)} %get-tuple-element.83), channel_id=1, source_target_pairs={{1,0},{2,1},{3,2},{4,3},{5,4},{6,5},{7,6},{8,7},{9,8},{10,9},{11,1... | collective-permute-start | bytes 6152 | tf_op jit(solution)/shard_map/ppermute | solution.py:29
  9.2 9.3 %collective-permute-start = (f32[1,512]{1,0:T(1,128)S(1)}, f32[1,512]{1,0:T(1,128)S(1)}, u32[]{:S(2)}, u32[]{:S(2)}) collective-permute-start(f32[1,512]{1,0:T(1,128)S(1)} %get-tuple-element.82), channel_id=1, source_target_pairs={{0,1},{1,2},{2,3},{3,4},{4,5},{5,6},{6,7},{7,8},{8,9},{9,10},{10,1... | collective-permute-start | bytes 6152 | tf_op jit(solution)/shard_map/ppermute | solution.py:28
  13.0 251.0 %collective-permute-start.9 = (f32[2,1,1,128]{3,2,1,0:T(1,128)S(1)}, f32[2,1,1,128]{3,2,1,0:T(1,128)S(1)}, u32[]{:S(2)}, u32[]{:S(2)}) collective-permute-start(f32[2,1,1,128]{3,2,1,0:T(1,128)S(1)} %get-tuple-element.75), channel_id=1, source_target_pairs={{8,0},{16,8},{24,16},{9,1},{17,9},{25,17},{10,2},{18,10},{26,18},{... | collective-permute-start | bytes 3080 | tf_op jit(solution)/shard_map/ppermute | solution.py:29
  14.4 249.5 %collective-permute-start.8 = (f32[2,1,1,128]{3,2,1,0:T(1,128)S(1)}, f32[2,1,1,128]{3,2,1,0:T(1,128)S(1)}, u32[]{:S(2)}, u32[]{:S(2)}) collective-permute-start(f32[2,1,1,128]{3,2,1,0:T(1,128)S(1)} %get-tuple-element.74), channel_id=1, source_target_pairs={{0,8},{8,16},{16,24},{1,9},{9,17},{17,25},{2,10},{10,18},{18,26},{... | collective-permute-start | bytes 3080 | tf_op jit(solution)/shard_map/ppermute | solution.py:28
  107.4 6.9 %collective-permute-start.5 = (f32[1,512]{1,0:T(1,128)S(1)}, f32[1,512]{1,0:T(1,128)S(1)}, u32[]{:S(2)}, u32[]{:S(2)}) collective-permute-start(f32[1,512]{1,0:T(1,128)S(1)} %get-tuple-element.81), channel_id=1, source_target_pairs={{1,0},{2,1},{3,2},{4,3},{5,4},{6,5},{7,6},{8,7},{9,8},{10,9},{11,1... | collective-permute-start | bytes 6152 | tf_op jit(solution)/shard_map/ppermute | solution.py:29
  110.6 3.7 collective-permute-start.4
  205.1 5.6 %collective-permute-start.7 = (f32[1,512]{1,0:T(1,128)S(1)}, f32[1,512]{1,0:T(1,128)S(1)}, u32[]{:S(2)}, u32[]{:S(2)}) collective-permute-start(f32[1,512]{1,0:T(1,128)S(1)} %get-tuple-element.79), channel_id=1, source_target_pairs={{1,0},{2,1},{3,2},{4,3},{5,4},{6,5},{7,6},{8,7},{9,8},{10,9},{11,1... | collective-permute-start | bytes 6152 | tf_op jit(solution)/shard_map/ppermute | solution.py:29
  258.4 11.2 %collective-permute-start.13 = (f32[1,512]{1,0:T(1,128)S(1)}, f32[1,512]{1,0:T(1,128)S(1)}, u32[]{:S(2)}, u32[]{:S(2)}) collective-permute-start(f32[1,512]{1,0:T(1,128)S(1)} %get-tuple-element.77), channel_id=1, source_target_pairs={{1,0},{2,1},{3,2},{4,3},{5,4},{6,5},{7,6},{8,7},{9,8},{10,9},{11,1... | collective-permute-start | bytes 6152 | tf_op jit(solution)/shard_map/ppermute | solution.py:29
  261.5 8.1 %collective-permute-start.12 = (f32[1,512]{1,0:T(1,128)S(1)}, f32[1,512]{1,0:T(1,128)S(1)}, u32[]{:S(2)}, u32[]{:S(2)}) collective-permute-start(f32[1,512]{1,0:T(1,128)S(1)} %get-tuple-element.76), channel_id=1, source_target_pairs={{0,1},{1,2},{2,3},{3,4},{4,5},{5,6},{6,7},{7,8},{8,9},{9,10},{10,1... | collective-permute-start | bytes 6152 | tf_op jit(solution)/shard_map/ppermute | solution.py:28
  264.0 189.1 %collective-permute-start.11 = (f32[2,1,66,128]{3,2,1,0:T(8,128)S(1)}, f32[2,1,66,128]{3,2,1,0:T(8,128)S(1)}, u32[]{:S(2)}, u32[]{:S(2)}) collective-permute-start(f32[2,1,66,128]{3,2,1,0:T(8,128)S(1)} %pad_maximum_fusion.4), channel_id=1, source_target_pairs={{1,0},{2,1},{3,2},{4,3},{5,4},{6,5},{7,6},{9,8},{10,9},{11,10},{12... | collective-permute-start | bytes 202760 | tf_op jit(solution)/shard_map/ppermute | solution.py:29
  265.9 187.2 %collective-permute-start.10 = (f32[2,1,66,128]{3,2,1,0:T(8,128)S(1)}, f32[2,1,66,128]{3,2,1,0:T(8,128)S(1)}, u32[]{:S(2)}, u32[]{:S(2)}) collective-permute-start(f32[2,1,66,128]{3,2,1,0:T(8,128)S(1)} %pad_maximum_fusion.4), channel_id=1, source_target_pairs={{0,1},{1,2},{2,3},{3,4},{4,5},{5,6},{6,7},{8,9},{9,10},{10,11},{11... | collective-permute-start | bytes 202760 | tf_op jit(solution)/shard_map/ppermute | solution.py:28
  453.5 7.2 %collective-permute-start.15 = (f32[2,1,1,128]{3,2,1,0:T(1,128)S(1)}, f32[2,1,1,128]{3,2,1,0:T(1,128)S(1)}, u32[]{:S(2)}, u32[]{:S(2)}) collective-permute-start(f32[2,1,1,128]{3,2,1,0:T(1,128)S(1)} %get-tuple-element.73), channel_id=1, source_target_pairs={{8,0},{16,8},{24,16},{9,1},{17,9},{25,17},{10,2},{18,10},{26,18},{... | collective-permute-start | bytes 3080 | tf_op jit(solution)/shard_map/ppermute | solution.py:29
  454.8 6.6 %collective-permute-start.14 = (f32[2,1,1,128]{3,2,1,0:T(1,128)S(1)}, f32[2,1,1,128]{3,2,1,0:T(1,128)S(1)}, u32[]{:S(2)}, u32[]{:S(2)}) collective-permute-start(f32[2,1,1,128]{3,2,1,0:T(1,128)S(1)} %get-tuple-element.72), channel_id=1, source_target_pairs={{0,8},{8,16},{16,24},{1,9},{9,17},{17,25},{2,10},{10,18},{18,26},{... | collective-permute-start | bytes 3080 | tf_op jit(solution)/shard_map/ppermute | solution.py:28
  461.5 5.7 %collective-permute-start.17 = (f32[2,1,66,128]{3,2,1,0:T(8,128)S(1)}, f32[2,1,66,128]{3,2,1,0:T(8,128)S(1)}, u32[]{:S(2)}, u32[]{:S(2)}) collective-permute-start(f32[2,1,66,128]{3,2,1,0:T(8,128)S(1)} %pad_maximum_fusion.5), channel_id=1, source_target_pairs={{1,0},{2,1},{3,2},{4,3},{5,4},{6,5},{7,6},{9,8},{10,9},{11,10},{12... | collective-permute-start | bytes 202760 | tf_op jit(solution)/shard_map/ppermute | solution.py:29
  464.4 4.0 collective-permute-start.16
  468.9 6.2 %collective-permute-start.19 = (f32[2,1,1,128]{3,2,1,0:T(1,128)S(1)}, f32[2,1,1,128]{3,2,1,0:T(1,128)S(1)}, u32[]{:S(2)}, u32[]{:S(2)}) collective-permute-start(f32[2,1,1,128]{3,2,1,0:T(1,128)S(1)} %get-tuple-element.71), channel_id=1, source_target_pairs={{8,0},{16,8},{24,16},{9,1},{17,9},{25,17},{10,2},{18,10},{26,18},{... | collective-permute-start | bytes 3080 | tf_op jit(solution)/shard_map/ppermute | solution.py:29
  470.2 5.6 %collective-permute-start.18 = (f32[2,1,1,128]{3,2,1,0:T(1,128)S(1)}, f32[2,1,1,128]{3,2,1,0:T(1,128)S(1)}, u32[]{:S(2)}, u32[]{:S(2)}) collective-permute-start(f32[2,1,1,128]{3,2,1,0:T(1,128)S(1)} %get-tuple-element.70), channel_id=1, source_target_pairs={{0,8},{8,16},{16,24},{1,9},{9,17},{17,25},{2,10},{10,18},{18,26},{... | collective-permute-start | bytes 3080 | tf_op jit(solution)/shard_map/ppermute | solution.py:28
  475.8 7.2 %collective-permute-start.21 = (f32[2,1,66,128]{3,2,1,0:T(8,128)S(1)}, f32[2,1,66,128]{3,2,1,0:T(8,128)S(1)}, u32[]{:S(2)}, u32[]{:S(2)}) collective-permute-start(f32[2,1,66,128]{3,2,1,0:T(8,128)S(1)} %pad_maximum_fusion.6), channel_id=1, source_target_pairs={{1,0},{2,1},{3,2},{4,3},{5,4},{6,5},{7,6},{9,8},{10,9},{11,10},{12... | collective-permute-start | bytes 202760 | tf_op jit(solution)/shard_map/ppermute | solution.py:29
  480.6 3.7 collective-permute-start.20
  484.8 6.5 %collective-permute-start.23 = (f32[2,1,1,128]{3,2,1,0:T(1,128)S(1)}, f32[2,1,1,128]{3,2,1,0:T(1,128)S(1)}, u32[]{:S(2)}, u32[]{:S(2)}) collective-permute-start(f32[2,1,1,128]{3,2,1,0:T(1,128)S(1)} %get-tuple-element.69), channel_id=1, source_target_pairs={{8,0},{16,8},{24,16},{9,1},{17,9},{25,17},{10,2},{18,10},{26,18},{... | collective-permute-start | bytes 3080 | tf_op jit(solution)/shard_map/ppermute | solution.py:29
  486.1 5.9 %collective-permute-start.22 = (f32[2,1,1,128]{3,2,1,0:T(1,128)S(1)}, f32[2,1,1,128]{3,2,1,0:T(1,128)S(1)}, u32[]{:S(2)}, u32[]{:S(2)}) collective-permute-start(f32[2,1,1,128]{3,2,1,0:T(1,128)S(1)} %get-tuple-element.68), channel_id=1, source_target_pairs={{0,8},{8,16},{16,24},{1,9},{9,17},{17,25},{2,10},{10,18},{18,26},{... | collective-permute-start | bytes 3080 | tf_op jit(solution)/shard_map/ppermute | solution.py:28
  492.0 7.2 %collective-permute-start.25 = (f32[2,1,66,128]{3,2,1,0:T(8,128)S(1)}, f32[2,1,66,128]{3,2,1,0:T(8,128)S(1)}, u32[]{:S(2)}, u32[]{:S(2)}) collective-permute-start(f32[2,1,66,128]{3,2,1,0:T(8,128)S(1)} %pad_maximum_fusion.7), channel_id=1, source_target_pairs={{1,0},{2,1},{3,2},{4,3},{5,4},{6,5},{7,6},{9,8},{10,9},{11,10},{12... | collective-permute-start | bytes 202760 | tf_op jit(solution)/shard_map/ppermute | solution.py:29
  (8 other events, 56.9 us)
where the time goes:
time: 508 us; the launch traced here: 502 us
  blocking collectives  228 us (45%)
  other arithmetic  177 us (35%)
  starting transfers between devices  78.9 us (16%)
  between operations  8.01 us (2%)
  waiting for transfers between devices  7.37 us (1%)
    unnamed x4, other arithmetic  171 us
    psum x3, blocking collectives, squares_sum(): return lax.psum(jnp.sum(residual * residual), ('magnet', 'slab'))  125 us
    psum x2, blocking collectives, local(): curvature = lax.psum(jnp.sum(direction * image_field), ('magnet', 'slab'))  90.7 us
    ppermute x13, starting transfers between devices, padded_2(): before = lax.ppermute(last, axis, up)  45.1 us
    ppermute x13, starting transfers between devices, padded_2(): after = lax.ppermute(initial, axis, down)  33.8 us
    all_gather x1, blocking collectives, local(): gathered = lax.all_gather(joule, 'slab', axis=0, tiled=True)  12.2 us
  transfers between devices with their start and end apart: 26, of which 10 were waited for; matrix products, arithmetic and copies ran while one was open for 35% of the time, Pallas kernels for 0%

commit v1 on v0

v1 whole, which is shorter than its diff:
```python
import functools

import jax
import jax.numpy as jnp
from jax import lax
from jax.experimental import pallas as pl
from jax.experimental.pallas import tpu as pltpu
from jax.sharding import PartitionSpec as P

MESH = pl.DeviceIdType.MESH
F32 = jnp.float32
leak_diag = 0.25
contact_gain = 4.0
copper_factor = 3.0
sheet_slope = 0.5
heat_factor = 1.5
time_step = 0.03
conduct_table = (0.3, 1.0, 2.0, 0.6)
capacity_table = (1.0, 1.5, 2.0, 1.2)
diffusivity_derivative = 0.4
REACH = 3
GRAM = ((0, 0), (0, 1), (0, 2), (0, 3), (1, 1), (1, 2), (1, 3), (2, 2), (2, 3))


def two_sum(a, b):
    s = a + b
    t = s - a
    return s, (a - (s - t)) + (b - t)


def halves(a):
    c = a * 4097.0
    high = c - (c - a)
    return high, a - high


def two_prod(a, b, sa, sb):
    p = a * b
    return p, ((sa[0] * sb[0] - p) + sa[0] * sb[1] + sa[1] * sb[0]) + sa[1] * sb[1]


def pair_add(x, y):
    s, e = two_sum(x[0], y[0])
    return s, e + (x[1] + y[1])


def tree(items, add):
    while len(items) > 1:
        items = [add(*items[i : i + 2]) if i + 1 < len(items) else items[i] for i in range(0, len(items), 2)]
    return items[0]


def pair_mul(x, y):
    p, e = two_prod(x[0], y[0], halves(x[0]), halves(y[0]))
    return p, e + (x[0] * y[1] + x[1] * y[0])


def quadratic(coefs, gram):
    terms = []
    for (i, j), g in gram.items():
        c = two_prod(coefs[i], coefs[j], halves(coefs[i]), halves(coefs[j]))
        terms.append(pair_mul(c, g))
    s = tree(terms, pair_add)
    return s[0] + s[1]


def lookup(kind, table):
    out = jnp.zeros(kind.shape, F32)
    for i, value in enumerate(table):
        out = jnp.where(kind == float(i), value, out)
    return out


def fluxes(temps, conds, first, last):
    rows = temps[0].shape[0]
    face = {}
    for i in range(first - 1, last):
        face[i] = (conds[i] + conds[i + 1]) * (temps[i + 1] - temps[i])
    out = []
    for i in range(first, last):
        t, k = temps[i], conds[i]
        total = face[i] - face[i - 1]
        for axis, size in ((0, rows), (1, t.shape[1])):
            f = (k + pltpu.roll(k, 1, axis)) * (pltpu.roll(t, 1, axis) - t)
            total = total + (f - pltpu.roll(f, size - 1, axis))
        out.append(0.5 * total)
    return out


def kernel(
    M, S, shells,
    warm_in, volt_in, pat_in, map_in, temp_in, kind_in,
    pot_out, brick_out,
    sheet_f, sheet_i, kind_v, first_b, later_b, onehot, red1, red2, heat_own, heat_ext, heat_b,
    local_sem, sheet_send, sheet_recv, len_send, len_recv, rad_send, rad_recv, late_send, late_recv,
    r1_send, r1_recv, r2_send, r2_recv, h_send, h_recv, e_send, e_recv,
):
    m = lax.axis_index("magnet")
    s = lax.axis_index("slab")
    rs, width = warm_in.shape
    rows, spokes = temp_in.shape[1], temp_in.shape[2]
    ext = 3 * rs
    brick = rows + 16
    g = m * S + s
    target0 = max(0, S - 2 - REACH)
    heated = s >= target0

    own_rows = pl.ds(pl.multiple_of(s * rs, 8), rs)
    mid = pl.ds(rs, rs)
    bmid = pl.ds(8, rows)
    zf = jnp.zeros((2, rs, width), F32)
    zi = jnp.zeros((2, rs, width), jnp.int32)
    for lo in (0, 2 * rs):
        sheet_f[:, lo : lo + rs, :] = zf
        sheet_i[:, lo : lo + rs, :] = zi
    ghost_t = jnp.zeros((brick, spokes), F32)
    ghost_k = jnp.full((brick, spokes), -1.0, F32)
    for buf in (first_b, later_b):
        for i in range(buf.shape[0]):
            buf[i, 0] = ghost_t
            buf[i, 1] = ghost_k
    local = [
        pltpu.make_async_copy(kind_in.at[0], kind_v, local_sem.at[0]),
        pltpu.make_async_copy(temp_in.at[0], first_b.at[1, 0, bmid, :], local_sem.at[1]),
        pltpu.make_async_copy(warm_in, sheet_f.at[0, mid, :], local_sem.at[2]),
        pltpu.make_async_copy(volt_in, sheet_f.at[1, mid, :], local_sem.at[3]),
        pltpu.make_async_copy(pat_in, sheet_i.at[0, mid, :], local_sem.at[4]),
        pltpu.make_async_copy(map_in.at[own_rows, :], sheet_i.at[1, mid, :], local_sem.at[5]),
    ]
    for c in local:
        c.start()

    barrier = pltpu.get_barrier_semaphore()

    def greet(who):
        pl.semaphore_signal(barrier, inc=1, device_id=who, device_id_type=MESH)

    for d in range(1, S):
        greet((m, lax.rem(s + d, S)))
    for d in range(1, M):
        greet((lax.rem(m + d, M), s))
    cross_up = (s == 0) & (m > 0)
    cross_down = (s == S - 1) & (m < M - 1)
    pl.when(cross_up)(lambda: greet((m - 1, S - 1)))
    pl.when(cross_down)(lambda: greet((m + 1, 0)))
    extra = jnp.where(cross_up | cross_down, 1, 0)
    for c in local:
        c.wait()
    first_b[1, 1, bmid, :] = kind_v[...].astype(F32)
    pl.semaphore_wait(barrier, S + M - 2 + extra)

    pending = []

    def sent(copies):
        for pred, c in copies:
            if pred is None:
                c.wait_send()
            else:
                pl.when(pred)(c.wait_send)

    def remote(pred, src, dst, send, recv, who):
        nonlocal pending
        c = pltpu.make_async_remote_copy(
            src_ref=src, dst_ref=dst, send_sem=send, recv_sem=recv, device_id=who, device_id_type=MESH
        )
        if pred is None:
            c.start()
        else:
            pl.when(pred)(c.start)
        pending.append((pred, c))

    def arrived(pred, src, dst, send, recv):
        c = pltpu.make_async_remote_copy(
            src_ref=src, dst_ref=dst, send_sem=send, recv_sem=recv, device_id=(m, s), device_id_type=MESH
        )
        if pred is None:
            c.wait_recv()
        else:
            pl.when(pred)(c.wait_recv)

    has_prev, has_next = g > 0, g < M * S - 1
    prev = (jnp.where(s == 0, m - 1, m), jnp.where(s == 0, S - 1, s - 1))
    nxt = (jnp.where(s == S - 1, m + 1, m), jnp.where(s == S - 1, 0, s + 1))
    before, after = pl.ds(0, rs), pl.ds(2 * rs, rs)
    for k, buf in enumerate((sheet_f, sheet_i)):
        remote(has_next, buf.at[:, mid, :], buf.at[:, before, :], sheet_send.at[2 * k], sheet_recv.at[2 * k], nxt)
        remote(has_prev, buf.at[:, mid, :], buf.at[:, after, :], sheet_send.at[2 * k + 1], sheet_recv.at[2 * k + 1], prev)
    layer = first_b.at[1]
    top_rows, end_rows = pl.ds(8, 8), pl.ds(rows, 8)
    top_halo, end_halo = pl.ds(0, 8), pl.ds(rows + 8, 8)
    remote(m < M - 1, layer.at[:, end_rows, :], layer.at[:, top_halo, :], len_send.at[0], len_recv.at[0], (m + 1, s))
    remote(m > 0, layer.at[:, top_rows, :], layer.at[:, end_halo, :], len_send.at[1], len_recv.at[1], (m - 1, s))

    lane_id = lax.broadcasted_iota(jnp.int32, (spokes, width), 0)
    base_cell = (shells - 2) * spokes
    cell_own = sheet_i[1, rs : 2 * rs, :] - base_cell
    upper_own = cell_own >= spokes
    col_own = jnp.where(upper_own, cell_own - spokes, cell_own)

    def put_onehot(at, row):
        onehot[at * spokes : (at + 1) * spokes, :] = jnp.where(lane_id == row, 1.0, 0.0).astype(jnp.bfloat16)

    for i in range(rs):
        put_onehot(i, col_own[i : i + 1, :])

    arrived(m > 0, layer.at[:, end_rows, :], layer.at[:, top_halo, :], len_send.at[0], len_recv.at[0])
    arrived(m < M - 1, layer.at[:, top_rows, :], layer.at[:, end_halo, :], len_send.at[1], len_recv.at[1])
    remote(s < S - 1, layer, first_b.at[0], rad_send.at[0], rad_recv.at[0], (m, s + 1))
    remote(s > 0, layer, first_b.at[2], rad_send.at[1], rad_recv.at[1], (m, s - 1))

    for k, buf in enumerate((sheet_f, sheet_i)):
        arrived(has_prev, buf.at[:, mid, :], buf.at[:, before, :], sheet_send.at[2 * k], sheet_recv.at[2 * k])
        arrived(has_next, buf.at[:, mid, :], buf.at[:, after, :], sheet_send.at[2 * k + 1], sheet_recv.at[2 * k + 1])

    pattern = sheet_i[0]
    row_id = lax.broadcasted_iota(jnp.int32, (ext, width), 0) + (g - 1) * rs
    col_id = lax.broadcasted_iota(jnp.int32, (ext, width), 1)
    valid = (row_id >= 0) & (row_id < M * S * rs)
    left_edge, right_edge = col_id == 0, col_id == width - 1

    def from_up(v):
        return pltpu.roll(v, 1, 0)

    def from_down(v):
        return pltpu.roll(v, ext - 1, 0)

    def from_left(v):
        return jnp.where(left_edge, 0.0, pltpu.roll(v, 1, 1))

    def from_right(v):
        return jnp.where(right_edge, 0.0, pltpu.roll(v, width - 1, 1))

    sides = (from_up, from_down, from_left, from_right)
    sigma = jnp.where(valid, jnp.where(pattern == 1, copper_factor, 1.0) / (1.0 + sheet_slope * sheet_f[0]), 0.0)
    coeffs = [0.5 * (sigma + side(sigma)) for side in sides]
    contact = jnp.where(pattern == 2, contact_gain, 0.0)
    diagonal = leak_diag + contact + coeffs[0] + coeffs[1] + coeffs[2] + coeffs[3]

    def apply(v):
        out = diagonal * v
        for c, side in zip(coeffs, sides):
            out = out - c * side(v)
        return jnp.where(valid, out, 0.0)

    basis = [jnp.where(valid, contact * sheet_f[1], 0.0)]
    for _ in range(3):
        basis.append(apply(basis[-1]))

    chunks = [[v[rs : 2 * rs, c : c + 128] for c in range(0, width, 128)] for v in basis]
    split = [[halves(v) for v in field] for field in chunks]
    highs, lows = [], []
    for i, j in GRAM:
        pairs = [two_prod(a, b, sa, sb) for a, b, sa, sb in zip(chunks[i], chunks[j], split[i], split[j])]
        p = tree(pairs, pair_add)
        for step in (4, 2, 1):
            p = pair_add(p, (pltpu.roll(p[0], step, 0), pltpu.roll(p[1], step, 0)))
        highs.append(p[0][0:1])
        lows.append(p[1][0:1])
    fill = [jnp.zeros((16 - len(GRAM), 128), F32)]
    red1[s] = jnp.concatenate(highs + fill + lows + fill, axis=0)
    for d in range(1, S):
        remote(None, red1.at[s], red1.at[s], r1_send.at[d], r1_recv.at[d], (m, lax.rem(s + d, S)))

    arrived(s > 0, layer, first_b.at[0], rad_send.at[0], rad_recv.at[0])
    arrived(s < S - 1, layer, first_b.at[2], rad_send.at[1], rad_recv.at[1])

    def conduct(temps, kinds):
        return [lookup(k, conduct_table) * (1.0 + diffusivity_derivative * t) for t, k in zip(temps, kinds)]

    def rate(kind):
        return lookup(kind, tuple(time_step / c for c in capacity_table))

    temps = [first_b[i, 0] for i in range(3)]
    kinds = [first_b[i, 1] for i in range(3)]
    (flux,) = fluxes(temps, conduct(temps, kinds), 1, 2)
    later_b[REACH, 0] = temps[1] + rate(kinds[1]) * flux
    later_b[REACH, 1] = kinds[1]
    early, pending = pending, []
    for d in range(1, REACH + 1):
        remote(s < S - d, later_b.at[REACH], later_b.at[REACH - d], late_send.at[2 * d - 2], late_recv.at[2 * d - 2], (m, s + d))
        remote(s >= d, later_b.at[REACH], later_b.at[REACH + d], late_send.at[2 * d - 1], late_recv.at[2 * d - 1], (m, s - d))

    late, pending = pending, []

    before_string = s == 0

    def outer(a):
        return jnp.where(before_string, pltpu.roll(a[0:rs], 3, 0), a[2 * rs :])

    cell_ext = outer(sheet_i[1]) - base_cell
    cell_ext = jnp.clip(cell_ext, 0, 2 * spokes - 1)
    upper_ext = cell_ext >= spokes
    col_ext = jnp.where(upper_ext, cell_ext - spokes, cell_ext)
    for i in range(3):
        put_onehot(rs + i, col_ext[i : i + 1, :])

    def pair_of(ref, i):
        return ref[i, 0:16], ref[i, 16:32]

    for d in range(1, S):
        src = lax.rem(s + S - d, S)
        arrived(None, red1.at[s], red1.at[src], r1_send.at[d], r1_recv.at[d])
    total = tree([pair_of(red1, i) for i in range(S)], pair_add)
    red2[m] = jnp.concatenate(total, axis=0)
    for d in range(1, M):
        remote(None, red2.at[m], red2.at[m], r2_send.at[d], r2_recv.at[d], (lax.rem(m + d, M), s))
    for d in range(1, M):
        src = lax.rem(m + M - d, M)
        arrived(None, red2.at[m], red2.at[src], r2_send.at[d], r2_recv.at[d])
    high, low = tree([pair_of(red2, i) for i in range(M)], pair_add)
    grid = 1024.0 * jnp.max(jnp.abs(high), axis=1, keepdims=True)
    coarse = (high + grid) - grid
    rest = jnp.sum((high - coarse) + low, axis=1, keepdims=True)
    sums = two_sum(jnp.sum(coarse, axis=1, keepdims=True), rest)
    gram = {ij: (sums[0][n : n + 1], sums[1][n : n + 1]) for n, ij in enumerate(GRAM)}

    def twice(x):
        return 2.0 * x[0], 2.0 * x[1]

    plain = {(i, j): gram[i, j] if i == j else twice(gram[i, j]) for i, j in GRAM if j < 3}
    with_a = {
        (0, 0): gram[0, 1],
        (0, 1): pair_add(gram[0, 2], gram[1, 1]),
        (1, 1): gram[1, 2],
        (0, 2): pair_add(gram[0, 3], gram[1, 2]),
        (1, 2): pair_add(gram[1, 3], gram[2, 2]),
        (2, 2): gram[2, 3],
    }

    def upto(table, n):
        return {ij: v for ij, v in table.items() if ij[1] < n}

    one = jnp.ones_like(gram[0, 0][0])
    norm0 = gram[0, 0][0]
    a0 = norm0 / gram[0, 1][0]
    norm1 = quadratic([one, -a0], upto(plain, 2))
    b1 = norm1 / norm0
    p1 = [1.0 + b1, -a0]
    a1 = norm1 / quadratic(p1, upto(with_a, 2))
    r2 = [one, -a0 - a1 * p1[0], -a1 * p1[1]]
    norm2 = quadratic(r2, plain)
    b2 = norm2 / norm1
    p2 = [r2[0] + b2 * p1[0], r2[1] + b2 * p1[1], r2[2]]
    a2 = norm2 / quadratic(p2, with_a)
    weights = [a0 + a1 * p1[0] + a2 * p2[0], a1 * p1[1] + a2 * p2[1], a2 * p2[2]]
    potential = weights[0] * basis[0] + weights[1] * basis[1] + weights[2] * basis[2]
    pot_out[...] = potential[rs : 2 * rs]

    joule = jnp.zeros_like(potential)
    for c, side in zip(coeffs, sides):
        drop = potential - side(potential)
        joule = joule + c * (drop * drop)
    joule = heat_factor * joule
    sub_id = lax.broadcasted_iota(jnp.int32, (rs, spokes), 0)

    def binned(power, upper, first, count):
        parts = []
        for value in (jnp.where(upper, 0.0, power), jnp.where(upper, power, 0.0)):
            for _ in range(3):
                part = value.astype(jnp.bfloat16).astype(F32)
                parts.append(part)
                value = value - part
        lhs = jnp.concatenate(parts, axis=0).astype(jnp.bfloat16)
        cols = onehot[first * spokes : (first + count) * spokes, :]
        out = lax.dot_general(lhs, cols, (((1,), (1,)), ((), ())), preferred_element_type=F32)
        heats = []
        for k in range(2):
            part = out[3 * k * rs : (3 * k + 1) * rs]
            part = part + out[(3 * k + 1) * rs : (3 * k + 2) * rs] + out[(3 * k + 2) * rs : (3 * k + 3) * rs]
            heat = jnp.zeros((rs, spokes), F32)
            for i in range(count):
                heat = jnp.where(sub_id == i, part[:, i * spokes : (i + 1) * spokes], heat)
            heats.append(heat)
        return heats

    lower, higher = binned(joule[rs : 2 * rs], upper_own, 0, rs)
    heat_own[0] = lower
    heat_own[1] = higher
    at = pl.ds(pl.multiple_of(8 + rs * s, 8), rs)
    for n, t in enumerate(range(target0, S)):
        remote(s != t, heat_own, heat_b.at[:, at, :], h_send.at[n], h_recv.at[s], (m, t))
    ext_lower, ext_higher = binned(outer(joule), upper_ext, rs, 3)
    heat_ext[0] = jnp.where(before_string, pltpu.roll(ext_lower, rs - 3, 0), ext_lower)
    heat_ext[1] = jnp.where(before_string, pltpu.roll(ext_higher, rs - 3, 0), ext_higher)
    for n, t in enumerate(range(target0, S)):
        remote((s == 0) & (s != t), heat_ext, heat_b.at[:, top_halo, :], e_send.at[n, 0], e_recv.at[0], (m, t))
        remote((s == S - 1) & (s != t), heat_ext, heat_b.at[:, end_halo, :], e_send.at[n, 1], e_recv.at[1], (m, t))

    @pl.when(heated)
    def _():
        heat_b[0, at, :] = lower
        heat_b[1, at, :] = higher

    @pl.when(s == S - 1)
    def _():
        heat_b[:, end_halo, :] = heat_ext[...]

    if target0 == 0:
        @pl.when(s == 0)
        def _():
            heat_b[:, top_halo, :] = heat_ext[...]

    for d in range(1, REACH + 1):
        arrived(s >= d, later_b.at[REACH], later_b.at[REACH - d], late_send.at[2 * d - 2], late_recv.at[2 * d - 2])
        arrived(s < S - d, later_b.at[REACH], later_b.at[REACH + d], late_send.at[2 * d - 1], late_recv.at[2 * d - 1])
    for j in range(S):
        part = heat_b.at[:, 8 + rs * j : 8 + rs * (j + 1), :]
        arrived(heated & (s != j), heat_own, part, h_send.at[0], h_recv.at[j])
    arrived(heated & (s != 0), heat_ext, heat_b.at[:, top_halo, :], e_send.at[0, 0], e_recv.at[0])
    arrived(heated & (s != S - 1), heat_ext, heat_b.at[:, end_halo, :], e_send.at[0, 1], e_recv.at[1])
    sent(late)
    for k in range(2):
        slot = REACH + (S - 2 + k) - s

        @pl.when((slot <= 2 * REACH) & (slot >= 0))
        def _():
            later_b[slot, 0] = later_b[slot, 0] + rate(later_b[slot, 1]) * heat_b[k]

    count = 2 * REACH + 1
    temps = [later_b[i, 0] for i in range(count)]
    kinds = [later_b[i, 1] for i in range(count)]
    heat_low, heat_high = heat_b[0], heat_b[1]
    for step in range(1, REACH + 1):
        conds = conduct(temps, kinds)
        flux = fluxes(temps, conds, step, count - step)
        for i, f in zip(range(step, count - step), flux):
            place = s + i - REACH
            heat = jnp.where(place == S - 2, heat_low, jnp.where(place == S - 1, heat_high, 0.0))
            temps[i] = temps[i] + rate(kinds[i]) * (f + heat)
    brick_out[0] = temps[REACH][8 : 8 + rows]
    sent(early + pending)


def solution(mesh):
    M, S = mesh.shape["magnet"], mesh.shape["slab"]

    def local(warm, volt, pattern, cells, temp, kind):
        rs, width = warm.shape
        depth, rows, spokes = temp.shape
        brick = rows + 16
        dma = pltpu.SemaphoreType.DMA
        targets = REACH + 2
        return pl.pallas_call(
            functools.partial(kernel, M, S, depth * S),
            out_shape=(
                jax.ShapeDtypeStruct((rs, width), F32),
                jax.ShapeDtypeStruct((depth, rows, spokes), F32),
            ),
            in_specs=[pl.BlockSpec(memory_space=pl.ANY)] * 6,
            out_specs=[pl.BlockSpec(memory_space=pltpu.VMEM)] * 2,
            scratch_shapes=[
                pltpu.VMEM((2, 3 * rs, width), F32),
                pltpu.VMEM((2, 3 * rs, width), jnp.int32),
                pltpu.VMEM((rows, spokes), jnp.int32),
                pltpu.VMEM((3, 2, brick, spokes), F32),
                pltpu.VMEM((2 * REACH + 1, 2, brick, spokes), F32),
                pltpu.VMEM(((rs + 3) * spokes, width), jnp.bfloat16),
                pltpu.VMEM((S, 32, 128), F32),
                pltpu.VMEM((M, 32, 128), F32),
                pltpu.VMEM((2, rs, spokes), F32),
                pltpu.VMEM((2, rs, spokes), F32),
                pltpu.VMEM((2, brick, spokes), F32),
                dma((6,)),
                dma((4,)), dma((4,)),
                dma((2,)), dma((2,)),
                dma((2,)), dma((2,)),
                dma((2 * REACH,)), dma((2 * REACH,)),
                dma((S,)), dma((S,)),
                dma((M,)), dma((M,)),
                dma((targets,)), dma((S,)),
                dma((targets, 2)), dma((2,)),
            ],
            compiler_params=pltpu.CompilerParams(
                collective_id=0, has_side_effects=True, vmem_limit_bytes=48 * 1024 * 1024
            ),
            name="window",
        )(warm, volt, pattern, cells, temp, kind)

    return jax.shard_map(
        local,
        mesh=mesh,
        in_specs=(
            P(("magnet", "slab"), None),
            P(("magnet", "slab"), None),
            P(("magnet", "slab"), None),
            P("magnet", None),
            P("slab", "magnet", None),
            P("slab", "magnet", None),
        ),
        out_specs=(P(("magnet", "slab"), None), P("slab", "magnet", None)),
        check_vma=False,
    )
```

time: 508 us -> 28 us (0.06); the launches traced: 502 us -> 27.5 us
  blocking collectives: 228 us -> 0 us
  other arithmetic: 177 us -> 0 us
  starting transfers between devices: 78.9 us -> 0 us
  Pallas kernels: 0 us -> 21 us
  waiting for transfers between devices: 7.37 us -> 0 us
  between operations: 8.01 us -> 0.65 us
    psum x5 -> x0, blocking collectives: 216 us -> none  [the longest x3 125 us: squares_sum(): return lax.psum(jnp.sum(residual * residual), ('magnet', 'slab'))]
    unnamed x4 -> x0, other arithmetic: 171 us -> none
    ppermute x26 -> x0, starting transfers between devices: 78.9 us -> none  [the longest x13 45.1 us: padded_2(): before = lax.ppermute(last, axis, up)]
    pallas_call x0 -> x1, Pallas kernels: none -> 21 us  [local(): pl.pallas_call(functools.partial(kernel, M, S, depth * S), out_shape=(jax...]
    all_gather x1 -> x0, blocking collectives: 12.2 us -> none  [local(): gathered = lax.all_gather(joule, 'slab', axis=0, tiled=True)]
    ppermute x26 -> x0, waiting for transfers between devices: 7.37 us -> none  [the longest x13 7.06 us: padded_2(): before = lax.ppermute(last, axis, up)]
  transfers between devices with their start and end apart: 26 -> 0, of which waited for: 10 -> 0; matrix products, arithmetic and copies ran while one was open for 35% -> 0% of each run, Pallas kernels for 0% -> 0%
where the time goes in v1:
time: 28 us; the launch traced here: 27.5 us
  Pallas kernels  21 us (75%)
  local copies, waits for them, and re-layouts  5.78 us (21%)
  between operations  0.65 us (2%)
    pallas_call x1, Pallas kernels, local(): pl.pallas_call(functools.partial(kernel, M, S, depth * S), out_shape=(jax...  21 us
    unnamed x14, local copies, waits for them, and re-layouts  5.78 us

profile of v1, /device:TPU:9, one launch (start us, length us, event | category | flops | bytes accessed | tf_op | source)
XLA Modules:
  0.0 27.5 jit_solution(11566512318627083728)
XLA Ops:
  0.6 0.0 copy-start
  0.6 0.9 %copy-done = s32[64,512]{1,0:T(8,128)S(1)} copy-done((s32[64,512]{1,0:T(8,128)S(1)}, s32[64,512]{1,0:T(8,128)}, u32[]{:S(2)}) %copy-start) | copy-done | bytes 131096
  1.5 0.0 copy-start.1
  1.5 0.8 %copy-done.1 = f32[1,64,128]{2,1,0:T(8,128)S(1)} copy-done((f32[1,64,128]{2,1,0:T(8,128)S(1)}, f32[1,64,128]{2,1,0:T(8,128)}, u32[]{:S(2)}) %copy-start.1) | copy-done | bytes 32792
  2.3 0.0 copy-start.2
  2.3 0.8 %copy-done.2 = s32[1,64,128]{2,1,0:T(8,128)S(1)} copy-done((s32[1,64,128]{2,1,0:T(8,128)S(1)}, s32[1,64,128]{2,1,0:T(8,128)}, u32[]{:S(2)}) %copy-start.2) | copy-done | bytes 32792
  3.1 0.0 copy-start.3
  3.1 0.7 %copy-done.3 = f32[8,512]{1,0:T(8,128)S(1)} copy-done((f32[8,512]{1,0:T(8,128)S(1)}, f32[8,512]{1,0:T(8,128)}, u32[]{:S(2)}) %copy-start.3) | copy-done | bytes 16408
  3.8 0.0 copy-start.4
  3.8 0.7 %copy-done.4 = f32[8,512]{1,0:T(8,128)S(1)} copy-done((f32[8,512]{1,0:T(8,128)S(1)}, f32[8,512]{1,0:T(8,128)}, u32[]{:S(2)}) %copy-start.4) | copy-done | bytes 16408
  4.5 0.0 copy-start.5
  4.5 0.7 %copy-done.5 = s32[8,512]{1,0:T(8,128)S(1)} copy-done((s32[8,512]{1,0:T(8,128)S(1)}, s32[8,512]{1,0:T(8,128)}, u32[]{:S(2)}) %copy-start.5) | copy-done | bytes 16408
  5.2 21.0 %window.1 = (f32[8,512]{1,0:T(8,128)S(1)}, f32[1,64,128]{2,1,0:T(8,128)S(1)}) custom-call(f32[8,512]{1,0:T(8,128)S(1)} %copy-done.3, f32[8,512]{1,0:T(8,128)S(1)} %copy-done.4, s32[8,512]{1,0:T(8,128)S(1)} %copy-done.5, s32[64,512]{1,0:T(8,128)S(1)} %copy-done, f32[1,64,128]{2,1,0:T(8,128)S(1)} %copy-done.1, s32[1,64,128]{2,1,0:T(8,128)S(1)} %copy-done.2), custom_call_target="tpu_custom_call" | custom-call | tf_op jit(solution)/shard_map/window/pallas_call | solution.py:443
  26.2 0.6 %copy.10 = f32[8,512]{1,0:T(8,128)} copy(f32[8,512]{1,0:T(8,128)S(1)} %get-tuple-element.4) | data formatting | bytes 32768
  26.8 0.6 %copy.11 = f32[1,64,128]{2,1,0:T(8,128)} copy(f32[1,64,128]{2,1,0:T(8,128)S(1)} %get-tuple-element.5) | data formatting | bytes 65536
Async XLA Ops:
  0.6 0.9 %copy-start = (s32[64,512]{1,0:T(8,128)S(1)}, s32[64,512]{1,0:T(8,128)}, u32[]{:S(2)}) copy-start(s32[64,512]{1,0:T(8,128)} %map_in.1) | copy-start | bytes 393220
  1.5 0.8 %copy-start.1 = (f32[1,64,128]{2,1,0:T(8,128)S(1)}, f32[1,64,128]{2,1,0:T(8,128)}, u32[]{:S(2)}) copy-start(f32[1,64,128]{2,1,0:T(8,128)} %temp_in.1) | copy-start | bytes 98308
  2.3 0.8 %copy-start.2 = (s32[1,64,128]{2,1,0:T(8,128)S(1)}, s32[1,64,128]{2,1,0:T(8,128)}, u32[]{:S(2)}) copy-start(s32[1,64,128]{2,1,0:T(8,128)} %kind_in.1) | copy-start | bytes 98308
  3.1 0.7 %copy-start.3 = (f32[8,512]{1,0:T(8,128)S(1)}, f32[8,512]{1,0:T(8,128)}, u32[]{:S(2)}) copy-start(f32[8,512]{1,0:T(8,128)} %warm_in.1) | copy-start | bytes 49156
  3.8 0.7 %copy-start.4 = (f32[8,512]{1,0:T(8,128)S(1)}, f32[8,512]{1,0:T(8,128)}, u32[]{:S(2)}) copy-start(f32[8,512]{1,0:T(8,128)} %volt_in.1) | copy-start | bytes 49156
  4.5 0.7 %copy-start.5 = (s32[8,512]{1,0:T(8,128)S(1)}, s32[8,512]{1,0:T(8,128)}, u32[]{:S(2)}) copy-start(s32[8,512]{1,0:T(8,128)} %pat_in.1) | copy-start | bytes 49156

commit v2 on v1

--- a/solution.py
+++ b/solution.py
@@ -276,10 +276,16 @@
     later_b[REACH, 0] = temps[1] + rate(kinds[1]) * flux
     later_b[REACH, 1] = kinds[1]
     early, pending = pending, []
+    def part(slot, d):
+        if d == 1:
+            return later_b.at[slot, 0]
+        return later_b.at[slot, :, bmid, :] if d == REACH else later_b.at[slot]
+
+    later_b[REACH - 1, 1] = kinds[0]
+    later_b[REACH + 1, 1] = kinds[2]
     for d in range(1, REACH + 1):
-        remote(s < S - d, later_b.at[REACH], later_b.at[REACH - d], late_send.at[2 * d - 2], late_recv.at[2 * d - 2], (m, s + d))
-        remote(s >= d, later_b.at[REACH], later_b.at[REACH + d], late_send.at[2 * d - 1], late_recv.at[2 * d - 1], (m, s - d))
-
+        remote(s < S - d, part(REACH, d), part(REACH - d, d), late_send.at[2 * d - 2], late_recv.at[2 * d - 2], (m, s + d))
+        remote(s >= d, part(REACH, d), part(REACH + d, d), late_send.at[2 * d - 1], late_recv.at[2 * d - 1], (m, s - d))
     late, pending = pending, []
 
     before_string = s == 0
@@ -401,8 +407,8 @@
             heat_b[:, top_halo, :] = heat_ext[...]
 
     for d in range(1, REACH + 1):
-        arrived(s >= d, later_b.at[REACH], later_b.at[REACH - d], late_send.at[2 * d - 2], late_recv.at[2 * d - 2])
-        arrived(s < S - d, later_b.at[REACH], later_b.at[REACH + d], late_send.at[2 * d - 1], late_recv.at[2 * d - 1])
+        arrived(s >= d, part(REACH, d), part(REACH - d, d), late_send.at[2 * d - 2], late_recv.at[2 * d - 2])
+        arrived(s < S - d, part(REACH, d), part(REACH + d, d), late_send.at[2 * d - 1], late_recv.at[2 * d - 1])
     for j in range(S):
         part = heat_b.at[:, 8 + rs * j : 8 + rs * (j + 1), :]
         arrived(heated & (s != j), heat_own, part, h_send.at[0], h_recv.at[j])
@@ -431,6 +437,14 @@
     sent(early + pending)
 
 
+def hand_over(pot, brick, pot_out, brick_out, sem):
+    copies = [pltpu.make_async_copy(pot, pot_out, sem.at[0]), pltpu.make_async_copy(brick, brick_out, sem.at[1])]
+    for c in copies:
+        c.start()
+    for c in copies:
+        c.wait()
+
+
 def solution(mesh):
     M, S = mesh.shape["magnet"], mesh.shape["slab"]
 
@@ -440,13 +454,14 @@
         brick = rows + 16
         dma = pltpu.SemaphoreType.DMA
         targets = REACH + 2
-        return pl.pallas_call(
+        shapes = (
+            jax.ShapeDtypeStruct((rs, width), F32),
+            jax.ShapeDtypeStruct((depth, rows, spokes), F32),
+        )
+        outs = pl.pallas_call(
             functools.partial(kernel, M, S, depth * S),
-            out_shape=(
-                jax.ShapeDtypeStruct((rs, width), F32),
-                jax.ShapeDtypeStruct((depth, rows, spokes), F32),
-            ),
-            in_specs=[pl.BlockSpec(memory_space=pl.ANY)] * 6,
+            out_shape=shapes,
+            in_specs=[pl.BlockSpec(memory_space=pltpu.HBM)] * 6,
             out_specs=[pl.BlockSpec(memory_space=pltpu.VMEM)] * 2,
             scratch_shapes=[
                 pltpu.VMEM((2, 3 * rs, width), F32),
@@ -471,10 +486,19 @@
                 dma((targets, 2)), dma((2,)),
             ],
             compiler_params=pltpu.CompilerParams(
-                collective_id=0, has_side_effects=True, vmem_limit_bytes=48 * 1024 * 1024
+                collective_id=0, has_side_effects=True, vmem_limit_bytes=63 * 1024 * 1024
             ),
             name="window",
         )(warm, volt, pattern, cells, temp, kind)
+        return pl.pallas_call(
+            hand_over,
+            out_shape=shapes,
+            in_specs=[pl.BlockSpec(memory_space=pltpu.HBM)] * 2,
+            out_specs=[pl.BlockSpec(memory_space=pltpu.HBM)] * 2,
+            scratch_shapes=[dma((2,))],
+            compiler_params=pltpu.CompilerParams(vmem_limit_bytes=63 * 1024 * 1024),
+            name="hand_over",
+        )(*outs)
 
     return jax.shard_map(
         local,

time: 28 us -> 25 us (0.89); the launches traced: 27.5 us -> 24.8 us
  local copies, waits for them, and re-layouts: 5.78 us -> 0 us
  Pallas kernels: 21 us -> 24.1 us
    unnamed x14 -> x0, local copies, waits for them, and re-layouts: 5.78 us -> none
    pallas_call x1 -> x2, Pallas kernels: 21 us -> 24.1 us  [the longest x1 21.5 us: local(): pl.pallas_call(functools.partial(kernel, M, S, depth * S), out_shape=shap...]
where the time goes in v2:
time: 25 us; the launch traced here: 24.8 us
  Pallas kernels  24.1 us (96%)
  between operations  0.64 us (3%)
    pallas_call x1, Pallas kernels, local(): pl.pallas_call(functools.partial(kernel, M, S, depth * S), out_shape=shap...  21.5 us
    pallas_call x1, Pallas kernels, local(): pl.pallas_call(hand_over, out_shape=shapes, in_specs=[pl.BlockSpec(memory...  2.61 us

profile of v2, /device:TPU:9, one launch (start us, length us, event | category | flops | bytes accessed | tf_op | source)
XLA Modules:
  0.0 24.8 jit_solution(12521501372628929795)
XLA Ops:
  0.6 21.5 %window.1 = (f32[8,512]{1,0:T(8,128)}, f32[1,64,128]{2,1,0:T(8,128)}) custom-call(f32[8,512]{1,0:T(8,128)} %warm_in.1, f32[8,512]{1,0:T(8,128)} %volt_in.1, s32[8,512]{1,0:T(8,128)} %pat_in.1, s32[64,512]{1,0:T(8,128)} %map_in.1, f32[1,64,128]{2,1,0:T(8,128)} %temp_in.1, s32[1,64,128]{2,1,0:T(8,128)} %kind_in.1), custom_call_target="tpu_custom_call" | custom-call | tf_op jit(solution)/shard_map/window/pallas_call | solution.py:461
  22.1 2.6 %hand_over.1 = (f32[8,512]{1,0:T(8,128)}, f32[1,64,128]{2,1,0:T(8,128)}) custom-call(f32[8,512]{1,0:T(8,128)} %get-tuple-element.4.pot, f32[1,64,128]{2,1,0:T(8,128)} %get-tuple-element.5.brick), custom_call_target="tpu_custom_call" | custom-call | tf_op jit(solution)/shard_map/hand_over/pallas_call | solution.py:493

commit v3 on v2

--- a/solution.py
+++ b/solution.py
@@ -91,7 +91,7 @@
     M, S, shells,
     warm_in, volt_in, pat_in, map_in, temp_in, kind_in,
     pot_out, brick_out,
-    sheet_f, sheet_i, kind_v, first_b, later_b, onehot, red1, red2, heat_own, heat_ext, heat_b,
+    sheet_f, sheet_i, kind_v, first_b, later_b, onehot, red1, red2, heat_own, heat_ext, heat_b, base_b, rate_b,
     local_sem, sheet_send, sheet_recv, len_send, len_recv, rad_send, rad_recv, late_send, late_recv,
     r1_send, r1_recv, r2_send, r2_recv, h_send, h_recv, e_send, e_recv,
 ):
@@ -119,6 +119,8 @@
         for i in range(buf.shape[0]):
             buf[i, 0] = ghost_t
             buf[i, 1] = ghost_k
+    for i in range(heat_b.shape[0]):
+        heat_b[i] = ghost_t
     local = [
         pltpu.make_async_copy(kind_in.at[0], kind_v, local_sem.at[0]),
         pltpu.make_async_copy(temp_in.at[0], first_b.at[1, 0, bmid, :], local_sem.at[1]),
@@ -248,16 +250,36 @@
 
     chunks = [[v[rs : 2 * rs, c : c + 128] for c in range(0, width, 128)] for v in basis]
     split = [[halves(v) for v in field] for field in chunks]
-    highs, lows = [], []
+    pairs = []
     for i, j in GRAM:
-        pairs = [two_prod(a, b, sa, sb) for a, b, sa, sb in zip(chunks[i], chunks[j], split[i], split[j])]
-        p = tree(pairs, pair_add)
-        for step in (4, 2, 1):
-            p = pair_add(p, (pltpu.roll(p[0], step, 0), pltpu.roll(p[1], step, 0)))
-        highs.append(p[0][0:1])
-        lows.append(p[1][0:1])
-    fill = [jnp.zeros((16 - len(GRAM), 128), F32)]
-    red1[s] = jnp.concatenate(highs + fill + lows + fill, axis=0)
+        terms = [two_prod(a, b, sa, sb) for a, b, sa, sb in zip(chunks[i], chunks[j], split[i], split[j])]
+        pairs.append(tree(terms, pair_add))
+    sub = lax.broadcasted_iota(jnp.int32, (8, 128), 0)
+    lane = lax.broadcasted_iota(jnp.int32, (8, 128), 1)
+
+    def folded(a, b, step):
+        first = (sub & step) == 0
+        near = jnp.where(first, a, b)
+        far = jnp.where(first, pltpu.roll(a, 8 - step, 0), pltpu.roll(b, step, 0))
+        return near, far
+
+    eight, ninth = pairs[:8], pairs[8]
+    for step in (4, 2, 1):
+        merged = []
+        for a, b in zip(eight[:step], eight[step:]):
+            parts = [folded(x, y, step) for x, y in zip(a, b)]
+            merged.append(pair_add((parts[0][0], parts[1][0]), (parts[0][1], parts[1][1])))
+        eight = merged
+
+    def fold_lanes(p):
+        for step in (64, 32):
+            p = pair_add(p, (pltpu.roll(p[0], step, 1), pltpu.roll(p[1], step, 1)))
+        return p
+
+    eight, ninth = fold_lanes(eight[0]), fold_lanes(ninth)
+    is_low = (lane & 32) != 0
+    both = [jnp.where(lane < 64, a, b) for a, b in zip(eight, ninth)]
+    red1[s] = jnp.where(is_low, both[1], both[0])
     for d in range(1, S):
         remote(None, red1.at[s], red1.at[s], r1_send.at[d], r1_recv.at[d], (m, lax.rem(s + d, S)))
 
@@ -301,24 +323,30 @@
         put_onehot(rs + i, col_ext[i : i + 1, :])
 
     def pair_of(ref, i):
-        return ref[i, 0:16], ref[i, 16:32]
+        tile = ref[i]
+        return tile, pltpu.roll(tile, 96, 1)
 
     for d in range(1, S):
         src = lax.rem(s + S - d, S)
         arrived(None, red1.at[s], red1.at[src], r1_send.at[d], r1_recv.at[d])
     total = tree([pair_of(red1, i) for i in range(S)], pair_add)
-    red2[m] = jnp.concatenate(total, axis=0)
+    red2[m] = jnp.where(is_low, pltpu.roll(total[1], 32, 1), total[0])
     for d in range(1, M):
         remote(None, red2.at[m], red2.at[m], r2_send.at[d], r2_recv.at[d], (lax.rem(m + d, M), s))
     for d in range(1, M):
         src = lax.rem(m + M - d, M)
         arrived(None, red2.at[m], red2.at[src], r2_send.at[d], r2_recv.at[d])
     high, low = tree([pair_of(red2, i) for i in range(M)], pair_add)
-    grid = 1024.0 * jnp.max(jnp.abs(high), axis=1, keepdims=True)
-    coarse = (high + grid) - grid
-    rest = jnp.sum((high - coarse) + low, axis=1, keepdims=True)
-    sums = two_sum(jnp.sum(coarse, axis=1, keepdims=True), rest)
-    gram = {ij: (sums[0][n : n + 1], sums[1][n : n + 1]) for n, ij in enumerate(GRAM)}
+    def added(high, low, axes):
+        grid = 1024.0 * jnp.max(jnp.abs(high), axis=axes, keepdims=True)
+        coarse = (high + grid) - grid
+        rest = jnp.sum((high - coarse) + low, axis=axes, keepdims=True)
+        return two_sum(jnp.sum(coarse, axis=axes, keepdims=True), rest)
+
+    in_eight, in_ninth = lane < 32, (lane >= 64) & (lane < 96)
+    sums = added(jnp.where(in_eight, high, 0.0), jnp.where(in_eight, low, 0.0), 1)
+    gram = {ij: (sums[0][n : n + 1], sums[1][n : n + 1]) for n, ij in enumerate(GRAM[:8])}
+    gram[GRAM[8]] = added(jnp.where(in_ninth, high, 0.0), jnp.where(in_ninth, low, 0.0), (0, 1))
 
     def twice(x):
         return 2.0 * x[0], 2.0 * x[1]
@@ -362,7 +390,7 @@
     def binned(power, upper, first, count):
         parts = []
         for value in (jnp.where(upper, 0.0, power), jnp.where(upper, power, 0.0)):
-            for _ in range(3):
+            for _ in range(2):
                 part = value.astype(jnp.bfloat16).astype(F32)
                 parts.append(part)
                 value = value - part
@@ -371,8 +399,7 @@
         out = lax.dot_general(lhs, cols, (((1,), (1,)), ((), ())), preferred_element_type=F32)
         heats = []
         for k in range(2):
-            part = out[3 * k * rs : (3 * k + 1) * rs]
-            part = part + out[(3 * k + 1) * rs : (3 * k + 2) * rs] + out[(3 * k + 2) * rs : (3 * k + 3) * rs]
+            part = out[2 * k * rs : (2 * k + 1) * rs] + out[(2 * k + 1) * rs : (2 * k + 2) * rs]
             heat = jnp.zeros((rs, spokes), F32)
             for i in range(count):
                 heat = jnp.where(sub_id == i, part[:, i * spokes : (i + 1) * spokes], heat)
@@ -383,66 +410,59 @@
     heat_own[0] = lower
     heat_own[1] = higher
     at = pl.ds(pl.multiple_of(8 + rs * s, 8), rs)
+
+    def slots(t):
+        return pl.ds(REACH + S - 2 - t, 2)
+
+    mine, pending = pending, []
     for n, t in enumerate(range(target0, S)):
-        remote(s != t, heat_own, heat_b.at[:, at, :], h_send.at[n], h_recv.at[s], (m, t))
+        remote(s != t, heat_own, heat_b.at[slots(t), at, :], h_send.at[n], h_recv.at[s], (m, t))
     ext_lower, ext_higher = binned(outer(joule), upper_ext, rs, 3)
     heat_ext[0] = jnp.where(before_string, pltpu.roll(ext_lower, rs - 3, 0), ext_lower)
     heat_ext[1] = jnp.where(before_string, pltpu.roll(ext_higher, rs - 3, 0), ext_higher)
+    at_end = (s == 0) | (s == S - 1)
+    side_of = jnp.where(before_string, 0, 1)
+    ext_at = pl.ds(pl.multiple_of(jnp.where(before_string, 0, rows + 8), 8), 8)
     for n, t in enumerate(range(target0, S)):
-        remote((s == 0) & (s != t), heat_ext, heat_b.at[:, top_halo, :], e_send.at[n, 0], e_recv.at[0], (m, t))
-        remote((s == S - 1) & (s != t), heat_ext, heat_b.at[:, end_halo, :], e_send.at[n, 1], e_recv.at[1], (m, t))
+        remote(at_end & (s != t), heat_ext, heat_b.at[slots(t), ext_at, :], e_send.at[n], e_recv.at[side_of], (m, t))
 
     @pl.when(heated)
     def _():
-        heat_b[0, at, :] = lower
-        heat_b[1, at, :] = higher
-
-    @pl.when(s == S - 1)
-    def _():
-        heat_b[:, end_halo, :] = heat_ext[...]
-
-    if target0 == 0:
-        @pl.when(s == 0)
+        slot = REACH + S - 2 - s
+        heat_b[slot, at, :] = lower
+        heat_b[slot + 1, at, :] = higher
+
+        @pl.when(at_end)
         def _():
-            heat_b[:, top_halo, :] = heat_ext[...]
+            heat_b[slot, ext_at, :] = heat_ext[0]
+            heat_b[slot + 1, ext_at, :] = heat_ext[1]
 
     for d in range(1, REACH + 1):
         arrived(s >= d, part(REACH, d), part(REACH - d, d), late_send.at[2 * d - 2], late_recv.at[2 * d - 2])
         arrived(s < S - d, part(REACH, d), part(REACH + d, d), late_send.at[2 * d - 1], late_recv.at[2 * d - 1])
+    count = 2 * REACH + 1
+    for i in range(count):
+        kind = later_b[i, 1]
+        base_b[i] = lookup(kind, conduct_table)
+        rate_b[i] = rate(kind)
+    sent(early + late + mine)
+    pair = pl.ds(0, 2)
     for j in range(S):
-        part = heat_b.at[:, 8 + rs * j : 8 + rs * (j + 1), :]
-        arrived(heated & (s != j), heat_own, part, h_send.at[0], h_recv.at[j])
-    arrived(heated & (s != 0), heat_ext, heat_b.at[:, top_halo, :], e_send.at[0, 0], e_recv.at[0])
-    arrived(heated & (s != S - 1), heat_ext, heat_b.at[:, end_halo, :], e_send.at[0, 1], e_recv.at[1])
-    sent(late)
-    for k in range(2):
-        slot = REACH + (S - 2 + k) - s
-
-        @pl.when((slot <= 2 * REACH) & (slot >= 0))
-        def _():
-            later_b[slot, 0] = later_b[slot, 0] + rate(later_b[slot, 1]) * heat_b[k]
+        at_j = pl.ds(8 + rs * j, rs)
+        arrived(heated & (s != j), heat_own, heat_b.at[pair, at_j, :], h_send.at[0], h_recv.at[j])
+    arrived(heated & (s != 0), heat_ext, heat_b.at[pair, top_halo, :], e_send.at[0], e_recv.at[0])
+    arrived(heated & (s != S - 1), heat_ext, heat_b.at[pair, end_halo, :], e_send.at[0], e_recv.at[1])
 
     count = 2 * REACH + 1
-    temps = [later_b[i, 0] for i in range(count)]
-    kinds = [later_b[i, 1] for i in range(count)]
-    heat_low, heat_high = heat_b[0], heat_b[1]
+    temps = [later_b[i, 0] + rate_b[i] * heat_b[i] for i in range(count)]
     for step in range(1, REACH + 1):
-        conds = conduct(temps, kinds)
-        flux = fluxes(temps, conds, step, count - step)
-        for i, f in zip(range(step, count - step), flux):
-            place = s + i - REACH
-            heat = jnp.where(place == S - 2, heat_low, jnp.where(place == S - 1, heat_high, 0.0))
-            temps[i] = temps[i] + rate(kinds[i]) * (f + heat)
+        first, last = step, count - step
+        near = range(first - 1, last + 1)
+        conds = {i: base_b[i] * (1.0 + diffusivity_derivative * temps[i]) for i in near}
+        for i, f in zip(range(first, last), fluxes(temps, conds, first, last)):
+            temps[i] = temps[i] + rate_b[i] * (f + heat_b[i])
     brick_out[0] = temps[REACH][8 : 8 + rows]
-    sent(early + pending)
-
-
-def hand_over(pot, brick, pot_out, brick_out, sem):
-    copies = [pltpu.make_async_copy(pot, pot_out, sem.at[0]), pltpu.make_async_copy(brick, brick_out, sem.at[1])]
-    for c in copies:
-        c.start()
-    for c in copies:
-        c.wait()
+    sent(pending)
 
 
 def solution(mesh):
@@ -458,7 +478,7 @@
             jax.ShapeDtypeStruct((rs, width), F32),
             jax.ShapeDtypeStruct((depth, rows, spokes), F32),
         )
-        outs = pl.pallas_call(
+        return pl.pallas_call(
             functools.partial(kernel, M, S, depth * S),
             out_shape=shapes,
             in_specs=[pl.BlockSpec(memory_space=pltpu.HBM)] * 6,
@@ -470,11 +490,13 @@
                 pltpu.VMEM((3, 2, brick, spokes), F32),
                 pltpu.VMEM((2 * REACH + 1, 2, brick, spokes), F32),
                 pltpu.VMEM(((rs + 3) * spokes, width), jnp.bfloat16),
-                pltpu.VMEM((S, 32, 128), F32),
-                pltpu.VMEM((M, 32, 128), F32),
+                pltpu.VMEM((S, 8, 128), F32),
+                pltpu.VMEM((M, 8, 128), F32),
                 pltpu.VMEM((2, rs, spokes), F32),
                 pltpu.VMEM((2, rs, spokes), F32),
-                pltpu.VMEM((2, brick, spokes), F32),
+                pltpu.VMEM((2 * REACH + 2, brick, spokes), F32),
+                pltpu.VMEM((2 * REACH + 1, brick, spokes), F32),
+                pltpu.VMEM((2 * REACH + 1, brick, spokes), F32),
                 dma((6,)),
                 dma((4,)), dma((4,)),
                 dma((2,)), dma((2,)),
@@ -483,22 +505,13 @@
                 dma((S,)), dma((S,)),
                 dma((M,)), dma((M,)),
                 dma((targets,)), dma((S,)),
-                dma((targets, 2)), dma((2,)),
+                dma((targets,)), dma((2,)),
             ],
             compiler_params=pltpu.CompilerParams(
                 collective_id=0, has_side_effects=True, vmem_limit_bytes=63 * 1024 * 1024
             ),
             name="window",
         )(warm, volt, pattern, cells, temp, kind)
-        return pl.pallas_call(
-            hand_over,
-            out_shape=shapes,
-            in_specs=[pl.BlockSpec(memory_space=pltpu.HBM)] * 2,
-            out_specs=[pl.BlockSpec(memory_space=pltpu.HBM)] * 2,
-            scratch_shapes=[dma((2,))],
-            compiler_params=pltpu.CompilerParams(vmem_limit_bytes=63 * 1024 * 1024),
-            name="hand_over",
-        )(*outs)
 
     return jax.shard_map(
         local,

time: 25 us -> 24.2 us (0.968)
  the two profiles are of different devices: /device:TPU:9 before, /device:TPU:0 now
where the time goes in v3:
time: 24.2 us; the launch traced here: 23.9 us
  Pallas kernels  21.4 us (88%)
  local copies, waits for them, and re-layouts  1.95 us (8%)
  between operations  0.65 us (3%)
    pallas_call x1, Pallas kernels, local(): pl.pallas_call(functools.partial(kernel, M, S, depth * S), out_shape=shap...  21.4 us
    unnamed x4, local copies, waits for them, and re-layouts  1.95 us

profile of v3, /device:TPU:0, one launch (start us, length us, event | category | flops | bytes accessed | tf_op | source)
XLA Modules:
  0.0 23.9 jit_solution(11879480800555393125)
XLA Ops:
  0.6 21.4 %window.1 = (f32[8,512]{1,0:T(8,128)}, f32[1,64,128]{2,1,0:T(8,128)}) custom-call(f32[8,512]{1,0:T(8,128)} %warm_in.1, f32[8,512]{1,0:T(8,128)} %volt_in.1, s32[8,512]{1,0:T(8,128)} %pat_in.1, s32[64,512]{1,0:T(8,128)} %map_in.1, f32[1,64,128]{2,1,0:T(8,128)} %temp_in.1, s32[1,64,128]{2,1,0:T(8,128)} %kind_in.1), custom_call_target="tpu_custom_call" | custom-call | tf_op jit(solution)/shard_map/window/pallas_call | solution.py:481
  22.0 0.0 copy-start
  22.0 1.3 %copy.10 = f32[8,512]{1,0:T(8,128)} copy(f32[8,512]{1,0:T(8,128)} %get-tuple-element.4) | data formatting | bytes 32768
  23.3 0.0 copy-done
  23.3 0.6 %copy.11 = f32[1,64,128]{2,1,0:T(8,128)} copy(f32[1,64,128]{2,1,0:T(8,128)S(1)} %copy-done) | data formatting | bytes 65536
Async XLA Ops:
  22.0 1.3 %copy-start = (f32[1,64,128]{2,1,0:T(8,128)S(1)}, f32[1,64,128]{2,1,0:T(8,128)}, u32[]{:S(2)}) copy-start(f32[1,64,128]{2,1,0:T(8,128)} %get-tuple-element.5) | copy-start | bytes 98308

commit v4 on v3

--- a/solution.py
+++ b/solution.py
@@ -92,6 +92,8 @@
     warm_in, volt_in, pat_in, map_in, temp_in, kind_in,
     pot_out, brick_out,
     sheet_f, sheet_i, kind_v, first_b, later_b, onehot, red1, red2, heat_own, heat_ext, heat_b, base_b, rate_b,
+    border_f, border_i, cross_f, cross_i,
+    border_send, border_recv, pass_send, pass_recv,
     local_sem, sheet_send, sheet_recv, len_send, len_recv, rad_send, rad_recv, late_send, late_recv,
     r1_send, r1_recv, r2_send, r2_recv, h_send, h_recv, e_send, e_recv,
 ):
@@ -99,7 +101,6 @@
     s = lax.axis_index("slab")
     rs, width = warm_in.shape
     rows, spokes = temp_in.shape[1], temp_in.shape[2]
-    ext = 3 * rs
     brick = rows + 16
     g = m * S + s
     target0 = max(0, S - 2 - REACH)
@@ -141,11 +142,17 @@
         greet((m, lax.rem(s + d, S)))
     for d in range(1, M):
         greet((lax.rem(m + d, M), s))
-    cross_up = (s == 0) & (m > 0)
-    cross_down = (s == S - 1) & (m < M - 1)
-    pl.when(cross_up)(lambda: greet((m - 1, S - 1)))
-    pl.when(cross_down)(lambda: greet((m + 1, 0)))
-    extra = jnp.where(cross_up | cross_down, 1, 0)
+    middle = S // 2 - 1
+    at_top, at_end = (s <= 1) & (m > 0), (s >= S - 2) & (m < M - 1)
+    is_middle = (s == middle) & (m < M - 1)
+    pl.when(at_top)(lambda: greet((m - 1, middle)))
+
+    @pl.when(is_middle)
+    def _():
+        greet((m + 1, 0))
+        greet((m + 1, 1))
+
+    extra = jnp.where(at_top, 1, 0) + jnp.where(is_middle, 2, 0)
     for c in local:
         c.wait()
     first_b[1, 1, bmid, :] = kind_v[...].astype(F32)
@@ -180,13 +187,20 @@
         else:
             pl.when(pred)(c.wait_recv)
 
-    has_prev, has_next = g > 0, g < M * S - 1
-    prev = (jnp.where(s == 0, m - 1, m), jnp.where(s == 0, S - 1, s - 1))
-    nxt = (jnp.where(s == S - 1, m + 1, m), jnp.where(s == S - 1, 0, s + 1))
+    has_prev, has_next = s > 0, s < S - 1
+    prev, nxt = (m, s - 1), (m, s + 1)
     before, after = pl.ds(0, rs), pl.ds(2 * rs, rs)
     for k, buf in enumerate((sheet_f, sheet_i)):
         remote(has_next, buf.at[:, mid, :], buf.at[:, before, :], sheet_send.at[2 * k], sheet_recv.at[2 * k], nxt)
         remote(has_prev, buf.at[:, mid, :], buf.at[:, after, :], sheet_send.at[2 * k + 1], sheet_recv.at[2 * k + 1], prev)
+    border_at = pl.ds(pl.multiple_of(jnp.where(at_top, 2 + s, jnp.where(at_end, s - (S - 2), 0)) * rs, 8), rs)
+    border_slot = jnp.where(at_top, 2 + s, jnp.where(at_end, s - (S - 2), 0))
+    border_to = (jnp.where(at_top, m - 1, m), middle)
+    for k, (buf, border) in enumerate(((sheet_f, border_f), (sheet_i, border_i))):
+        remote(
+            at_top | at_end, buf.at[:, mid, :], border.at[:, border_at, :],
+            border_send.at[k], border_recv.at[k, border_slot], border_to,
+        )
     layer = first_b.at[1]
     top_rows, end_rows = pl.ds(8, 8), pl.ds(rows, 8)
     top_halo, end_halo = pl.ds(0, 8), pl.ds(rows + 8, 8)
@@ -214,48 +228,44 @@
         arrived(has_prev, buf.at[:, mid, :], buf.at[:, before, :], sheet_send.at[2 * k], sheet_recv.at[2 * k])
         arrived(has_next, buf.at[:, mid, :], buf.at[:, after, :], sheet_send.at[2 * k + 1], sheet_recv.at[2 * k + 1])
 
-    pattern = sheet_i[0]
-    row_id = lax.broadcasted_iota(jnp.int32, (ext, width), 0) + (g - 1) * rs
-    col_id = lax.broadcasted_iota(jnp.int32, (ext, width), 1)
-    valid = (row_id >= 0) & (row_id < M * S * rs)
-    left_edge, right_edge = col_id == 0, col_id == width - 1
-
-    def from_up(v):
-        return pltpu.roll(v, 1, 0)
-
-    def from_down(v):
-        return pltpu.roll(v, ext - 1, 0)
-
-    def from_left(v):
-        return jnp.where(left_edge, 0.0, pltpu.roll(v, 1, 1))
-
-    def from_right(v):
-        return jnp.where(right_edge, 0.0, pltpu.roll(v, width - 1, 1))
-
-    sides = (from_up, from_down, from_left, from_right)
-    sigma = jnp.where(valid, jnp.where(pattern == 1, copper_factor, 1.0) / (1.0 + sheet_slope * sheet_f[0]), 0.0)
-    coeffs = [0.5 * (sigma + side(sigma)) for side in sides]
-    contact = jnp.where(pattern == 2, contact_gain, 0.0)
-    diagonal = leak_diag + contact + coeffs[0] + coeffs[1] + coeffs[2] + coeffs[3]
-
-    def apply(v):
-        out = diagonal * v
-        for c, side in zip(coeffs, sides):
-            out = out - c * side(v)
-        return jnp.where(valid, out, 0.0)
-
-    basis = [jnp.where(valid, contact * sheet_f[1], 0.0)]
-    for _ in range(3):
-        basis.append(apply(basis[-1]))
-
-    chunks = [[v[rs : 2 * rs, c : c + 128] for c in range(0, width, 128)] for v in basis]
-    split = [[halves(v) for v in field] for field in chunks]
-    pairs = []
-    for i, j in GRAM:
-        terms = [two_prod(a, b, sa, sb) for a, b, sa, sb in zip(chunks[i], chunks[j], split[i], split[j])]
-        pairs.append(tree(terms, pair_add))
+    def field_steps(n, first_row):
+        row_id = lax.broadcasted_iota(jnp.int32, (n, width), 0) + first_row
+        col_id = lax.broadcasted_iota(jnp.int32, (n, width), 1)
+        valid = (row_id >= 0) & (row_id < M * S * rs)
+        left_edge, right_edge = col_id == 0, col_id == width - 1
+
+        def from_up(v):
+            return pltpu.roll(v, 1, 0)
+
+        def from_down(v):
+            return pltpu.roll(v, n - 1, 0)
+
+        def from_left(v):
+            return jnp.where(left_edge, 0.0, pltpu.roll(v, 1, 1))
+
+        def from_right(v):
+            return jnp.where(right_edge, 0.0, pltpu.roll(v, width - 1, 1))
+
+        return valid, (from_up, from_down, from_left, from_right)
+
+    def krylov(warm, volt, pattern, first_row, count):
+        valid, sides = field_steps(warm.shape[0], first_row)
+        sigma = jnp.where(valid, jnp.where(pattern == 1, copper_factor, 1.0) / (1.0 + sheet_slope * warm), 0.0)
+        coeffs = [0.5 * (sigma + side(sigma)) for side in sides]
+        contact = jnp.where(pattern == 2, contact_gain, 0.0)
+        diagonal = leak_diag + contact + coeffs[0] + coeffs[1] + coeffs[2] + coeffs[3]
+        basis = [jnp.where(valid, contact * volt, 0.0)]
+        for _ in range(count - 1):
+            v = basis[-1]
+            out = diagonal * v
+            for c, side in zip(coeffs, sides):
+                out = out - c * side(v)
+            basis.append(jnp.where(valid, out, 0.0))
+        return coeffs, sides, basis
+
     sub = lax.broadcasted_iota(jnp.int32, (8, 128), 0)
     lane = lax.broadcasted_iota(jnp.int32, (8, 128), 1)
+    is_low = (lane & 32) != 0
 
     def folded(a, b, step):
         first = (sub & step) == 0
@@ -263,23 +273,57 @@
         far = jnp.where(first, pltpu.roll(a, 8 - step, 0), pltpu.roll(b, step, 0))
         return near, far
 
-    eight, ninth = pairs[:8], pairs[8]
-    for step in (4, 2, 1):
-        merged = []
-        for a, b in zip(eight[:step], eight[step:]):
-            parts = [folded(x, y, step) for x, y in zip(a, b)]
-            merged.append(pair_add((parts[0][0], parts[1][0]), (parts[0][1], parts[1][1])))
-        eight = merged
-
     def fold_lanes(p):
         for step in (64, 32):
             p = pair_add(p, (pltpu.roll(p[0], step, 1), pltpu.roll(p[1], step, 1)))
         return p
 
-    eight, ninth = fold_lanes(eight[0]), fold_lanes(ninth)
-    is_low = (lane & 32) != 0
-    both = [jnp.where(lane < 64, a, b) for a, b in zip(eight, ninth)]
-    red1[s] = jnp.where(is_low, both[1], both[0])
+    def unpacked(tile):
+        return tile, pltpu.roll(tile, 96, 1)
+
+    def packed(p):
+        return jnp.where(is_low, pltpu.roll(p[1], 32, 1), p[0])
+
+    def gram_tile(basis, lo, hi):
+        cells = [(r, c) for r in range(lo, hi, 8) for c in range(0, width, 128)]
+        chunks = [[v[r : r + 8, c : c + 128] for r, c in cells] for v in basis]
+        split = [[halves(v) for v in field] for field in chunks]
+        pairs = []
+        for i, j in GRAM:
+            terms = [two_prod(a, b, sa, sb) for a, b, sa, sb in zip(chunks[i], chunks[j], split[i], split[j])]
+            pairs.append(tree(terms, pair_add))
+        eight, ninth = pairs[:8], pairs[8]
+        for step in (4, 2, 1):
+            merged = []
+            for a, b in zip(eight[:step], eight[step:]):
+                parts = [folded(x, y, step) for x, y in zip(a, b)]
+                merged.append(pair_add((parts[0][0], parts[1][0]), (parts[0][1], parts[1][1])))
+            eight = merged
+        eight, ninth = fold_lanes(eight[0]), fold_lanes(ninth)
+        both = [jnp.where(lane < 64, a, b) for a, b in zip(eight, ninth)]
+        return jnp.where(is_low, both[1], both[0])
+
+    _, _, basis = krylov(sheet_f[0], sheet_f[1], sheet_i[0], (g - 1) * rs, 4)
+    cross_up, cross_down = (s == 0) & (m > 0), (s == S - 1) & (m < M - 1)
+    is_cross = cross_up | cross_down
+    red1[s] = jnp.where(is_cross, 0.0, gram_tile(basis, rs, 2 * rs))
+
+    @pl.when(is_middle)
+    def _():
+        for k, (buf, border) in enumerate(((sheet_f, border_f), (sheet_i, border_i))):
+            for slot in range(4):
+                arrived(None, buf.at[:, mid, :], border.at[:, slot * rs : (slot + 1) * rs, :], border_send.at[k], border_recv.at[k, slot])
+
+    for k, (border, cross) in enumerate(((border_f, cross_f), (border_i, cross_i))):
+        remote(is_middle, border.at[:, 2 * rs : 3 * rs, :], cross, pass_send.at[k, 0], pass_recv.at[k], (m, S - 1))
+        remote(is_middle, border.at[:, rs : 2 * rs, :], cross, pass_send.at[k, 1], pass_recv.at[k], (m + 1, 0))
+
+    @pl.when(is_middle)
+    def _():
+        _, _, fields = krylov(border_f[0], border_f[1], border_i[0], (m * S + S - 2) * rs, 4)
+        tile = gram_tile(fields, rs, 3 * rs)
+        red1[s] = packed(pair_add(unpacked(red1[s]), unpacked(tile)))
+
     for d in range(1, S):
         remote(None, red1.at[s], red1.at[s], r1_send.at[d], r1_recv.at[d], (m, lax.rem(s + d, S)))
 
@@ -310,6 +354,31 @@
         remote(s >= d, part(REACH, d), part(REACH + d, d), late_send.at[2 * d - 1], late_recv.at[2 * d - 1], (m, s - d))
     late, pending = pending, []
 
+    def pair_of(ref, i):
+        return unpacked(ref[i])
+
+    for d in range(1, S):
+        src = lax.rem(s + S - d, S)
+        arrived(None, red1.at[s], red1.at[src], r1_send.at[d], r1_recv.at[d])
+    total = tree([pair_of(red1, i) for i in range(S)], pair_add)
+    red2[m] = packed(total)
+    for d in range(1, M):
+        remote(None, red2.at[m], red2.at[m], r2_send.at[d], r2_recv.at[d], (lax.rem(m + d, M), s))
+    for k, (border, cross) in enumerate(((border_f, cross_f), (border_i, cross_i))):
+        arrived(is_cross, border.at[:, before, :], cross, pass_send.at[k, 0], pass_recv.at[k])
+
+    @pl.when(cross_up)
+    def _():
+        sheet_f[:, before, :] = cross_f[...]
+        sheet_i[:, before, :] = cross_i[...]
+
+    @pl.when(cross_down)
+    def _():
+        sheet_f[:, after, :] = cross_f[...]
+        sheet_i[:, after, :] = cross_i[...]
+
+    coeffs, sides, basis = krylov(sheet_f[0], sheet_f[1], sheet_i[0], (g - 1) * rs, 3)
+
     before_string = s == 0
 
     def outer(a):
@@ -322,17 +391,6 @@
     for i in range(3):
         put_onehot(rs + i, col_ext[i : i + 1, :])
 
-    def pair_of(ref, i):
-        tile = ref[i]
-        return tile, pltpu.roll(tile, 96, 1)
-
-    for d in range(1, S):
-        src = lax.rem(s + S - d, S)
-        arrived(None, red1.at[s], red1.at[src], r1_send.at[d], r1_recv.at[d])
-    total = tree([pair_of(red1, i) for i in range(S)], pair_add)
-    red2[m] = jnp.where(is_low, pltpu.roll(total[1], 32, 1), total[0])
-    for d in range(1, M):
-        remote(None, red2.at[m], red2.at[m], r2_send.at[d], r2_recv.at[d], (lax.rem(m + d, M), s))
     for d in range(1, M):
         src = lax.rem(m + M - d, M)
         arrived(None, red2.at[m], red2.at[src], r2_send.at[d], r2_recv.at[d])
@@ -420,11 +478,11 @@
     ext_lower, ext_higher = binned(outer(joule), upper_ext, rs, 3)
     heat_ext[0] = jnp.where(before_string, pltpu.roll(ext_lower, rs - 3, 0), ext_lower)
     heat_ext[1] = jnp.where(before_string, pltpu.roll(ext_higher, rs - 3, 0), ext_higher)
-    at_end = (s == 0) | (s == S - 1)
+    at_rim = (s == 0) | (s == S - 1)
     side_of = jnp.where(before_string, 0, 1)
     ext_at = pl.ds(pl.multiple_of(jnp.where(before_string, 0, rows + 8), 8), 8)
     for n, t in enumerate(range(target0, S)):
-        remote(at_end & (s != t), heat_ext, heat_b.at[slots(t), ext_at, :], e_send.at[n], e_recv.at[side_of], (m, t))
+        remote(at_rim & (s != t), heat_ext, heat_b.at[slots(t), ext_at, :], e_send.at[n], e_recv.at[side_of], (m, t))
 
     @pl.when(heated)
     def _():
@@ -432,7 +490,7 @@
         heat_b[slot, at, :] = lower
         heat_b[slot + 1, at, :] = higher
 
-        @pl.when(at_end)
+        @pl.when(at_rim)
         def _():
             heat_b[slot, ext_at, :] = heat_ext[0]
             heat_b[slot + 1, ext_at, :] = heat_ext[1]
@@ -497,6 +555,12 @@
                 pltpu.VMEM((2 * REACH + 2, brick, spokes), F32),
                 pltpu.VMEM((2 * REACH + 1, brick, spokes), F32),
                 pltpu.VMEM((2 * REACH + 1, brick, spokes), F32),
+                pltpu.VMEM((2, 4 * rs, width), F32),
+                pltpu.VMEM((2, 4 * rs, width), jnp.int32),
+                pltpu.VMEM((2, rs, width), F32),
+                pltpu.VMEM((2, rs, width), jnp.int32),
+                dma((2,)), dma((2, 4)),
+                dma((2, 2)), dma((2,)),
                 dma((6,)),
                 dma((4,)), dma((4,)),
                 dma((2,)), dma((2,)),

time: 24.2 us -> 23.4 us (0.967)
  the two profiles are of different devices: /device:TPU:0 before, /device:TPU:9 now
where the time goes in v4:
time: 23.4 us; the launch traced here: 23.1 us
  Pallas kernels  20.5 us (88%)
  local copies, waits for them, and re-layouts  1.95 us (8%)
  between operations  0.65 us (3%)
    pallas_call x1, Pallas kernels, local(): pl.pallas_call(functools.partial(kernel, M, S, depth * S), out_shape=shap...  20.5 us
    unnamed x4, local copies, waits for them, and re-layouts  1.95 us

profile of v4, /device:TPU:9, one launch (start us, length us, event | category | flops | bytes accessed | tf_op | source)
XLA Modules:
  0.0 23.1 jit_solution(7880064189454811012)
XLA Ops:
  0.6 20.5 %window.1 = (f32[8,512]{1,0:T(8,128)}, f32[1,64,128]{2,1,0:T(8,128)}) custom-call(f32[8,512]{1,0:T(8,128)} %warm_in.1, f32[8,512]{1,0:T(8,128)} %volt_in.1, s32[8,512]{1,0:T(8,128)} %pat_in.1, s32[64,512]{1,0:T(8,128)} %map_in.1, f32[1,64,128]{2,1,0:T(8,128)} %temp_in.1, s32[1,64,128]{2,1,0:T(8,128)} %kind_in.1), custom_call_target="tpu_custom_call" | custom-call | tf_op jit(solution)/shard_map/window/pallas_call | solution.py:539
  21.2 0.0 copy-start
  21.2 1.3 %copy.10 = f32[8,512]{1,0:T(8,128)} copy(f32[8,512]{1,0:T(8,128)} %get-tuple-element.4) | data formatting | bytes 32768
  22.5 0.0 copy-done
  22.5 0.6 %copy.11 = f32[1,64,128]{2,1,0:T(8,128)} copy(f32[1,64,128]{2,1,0:T(8,128)S(1)} %copy-done) | data formatting | bytes 65536
Async XLA Ops:
  21.2 1.3 %copy-start = (f32[1,64,128]{2,1,0:T(8,128)S(1)}, f32[1,64,128]{2,1,0:T(8,128)}, u32[]{:S(2)}) copy-start(f32[1,64,128]{2,1,0:T(8,128)} %get-tuple-element.5) | copy-start | bytes 98308

commit v5 on v4

--- a/solution.py
+++ b/solution.py
@@ -91,8 +91,8 @@
     M, S, shells,
     warm_in, volt_in, pat_in, map_in, temp_in, kind_in,
     pot_out, brick_out,
-    sheet_f, sheet_i, kind_v, first_b, later_b, onehot, red1, red2, heat_own, heat_ext, heat_b, base_b, rate_b,
-    border_f, border_i, cross_f, cross_i,
+    sheet, ints, kind_v, first_b, later_b, onehot, red1, red2, heat_own, heat_ext, heat_b, base_b, rate_b,
+    border, cross,
     border_send, border_recv, pass_send, pass_recv,
     local_sem, sheet_send, sheet_recv, len_send, len_recv, rad_send, rad_recv, late_send, late_recv,
     r1_send, r1_recv, r2_send, r2_recv, h_send, h_recv, e_send, e_recv,
@@ -109,11 +109,8 @@
     own_rows = pl.ds(pl.multiple_of(s * rs, 8), rs)
     mid = pl.ds(rs, rs)
     bmid = pl.ds(8, rows)
-    zf = jnp.zeros((2, rs, width), F32)
-    zi = jnp.zeros((2, rs, width), jnp.int32)
     for lo in (0, 2 * rs):
-        sheet_f[:, lo : lo + rs, :] = zf
-        sheet_i[:, lo : lo + rs, :] = zi
+        sheet[:, lo : lo + rs, :] = jnp.zeros((4, rs, width), F32)
     ghost_t = jnp.zeros((brick, spokes), F32)
     ghost_k = jnp.full((brick, spokes), -1.0, F32)
     for buf in (first_b, later_b):
@@ -125,10 +122,10 @@
     local = [
         pltpu.make_async_copy(kind_in.at[0], kind_v, local_sem.at[0]),
         pltpu.make_async_copy(temp_in.at[0], first_b.at[1, 0, bmid, :], local_sem.at[1]),
-        pltpu.make_async_copy(warm_in, sheet_f.at[0, mid, :], local_sem.at[2]),
-        pltpu.make_async_copy(volt_in, sheet_f.at[1, mid, :], local_sem.at[3]),
-        pltpu.make_async_copy(pat_in, sheet_i.at[0, mid, :], local_sem.at[4]),
-        pltpu.make_async_copy(map_in.at[own_rows, :], sheet_i.at[1, mid, :], local_sem.at[5]),
+        pltpu.make_async_copy(warm_in, sheet.at[0, mid, :], local_sem.at[2]),
+        pltpu.make_async_copy(volt_in, sheet.at[1, mid, :], local_sem.at[3]),
+        pltpu.make_async_copy(pat_in, ints.at[0], local_sem.at[4]),
+        pltpu.make_async_copy(map_in.at[own_rows, :], ints.at[1], local_sem.at[5]),
     ]
     for c in local:
         c.start()
@@ -155,6 +152,7 @@
     extra = jnp.where(at_top, 1, 0) + jnp.where(is_middle, 2, 0)
     for c in local:
         c.wait()
+    sheet[2:4, rs : 2 * rs, :] = ints[...].astype(F32)
     first_b[1, 1, bmid, :] = kind_v[...].astype(F32)
     pl.semaphore_wait(barrier, S + M - 2 + extra)
 
@@ -190,17 +188,15 @@
     has_prev, has_next = s > 0, s < S - 1
     prev, nxt = (m, s - 1), (m, s + 1)
     before, after = pl.ds(0, rs), pl.ds(2 * rs, rs)
-    for k, buf in enumerate((sheet_f, sheet_i)):
-        remote(has_next, buf.at[:, mid, :], buf.at[:, before, :], sheet_send.at[2 * k], sheet_recv.at[2 * k], nxt)
-        remote(has_prev, buf.at[:, mid, :], buf.at[:, after, :], sheet_send.at[2 * k + 1], sheet_recv.at[2 * k + 1], prev)
+    remote(has_next, sheet.at[:, mid, :], sheet.at[:, before, :], sheet_send.at[0], sheet_recv.at[0], nxt)
+    remote(has_prev, sheet.at[:, mid, :], sheet.at[:, after, :], sheet_send.at[1], sheet_recv.at[1], prev)
     border_at = pl.ds(pl.multiple_of(jnp.where(at_top, 2 + s, jnp.where(at_end, s - (S - 2), 0)) * rs, 8), rs)
     border_slot = jnp.where(at_top, 2 + s, jnp.where(at_end, s - (S - 2), 0))
     border_to = (jnp.where(at_top, m - 1, m), middle)
-    for k, (buf, border) in enumerate(((sheet_f, border_f), (sheet_i, border_i))):
-        remote(
-            at_top | at_end, buf.at[:, mid, :], border.at[:, border_at, :],
-            border_send.at[k], border_recv.at[k, border_slot], border_to,
-        )
+    remote(
+        at_top | at_end, sheet.at[:, mid, :], border.at[:, border_at, :],
+        border_send.at[0], border_recv.at[border_slot], border_to,
+    )
     layer = first_b.at[1]
     top_rows, end_rows = pl.ds(8, 8), pl.ds(rows, 8)
     top_halo, end_halo = pl.ds(0, 8), pl.ds(rows + 8, 8)
@@ -209,7 +205,7 @@
 
     lane_id = lax.broadcasted_iota(jnp.int32, (spokes, width), 0)
     base_cell = (shells - 2) * spokes
-    cell_own = sheet_i[1, rs : 2 * rs, :] - base_cell
+    cell_own = ints[1] - base_cell
     upper_own = cell_own >= spokes
     col_own = jnp.where(upper_own, cell_own - spokes, cell_own)
 
@@ -219,14 +215,8 @@
     for i in range(rs):
         put_onehot(i, col_own[i : i + 1, :])
 
-    arrived(m > 0, layer.at[:, end_rows, :], layer.at[:, top_halo, :], len_send.at[0], len_recv.at[0])
-    arrived(m < M - 1, layer.at[:, top_rows, :], layer.at[:, end_halo, :], len_send.at[1], len_recv.at[1])
-    remote(s < S - 1, layer, first_b.at[0], rad_send.at[0], rad_recv.at[0], (m, s + 1))
-    remote(s > 0, layer, first_b.at[2], rad_send.at[1], rad_recv.at[1], (m, s - 1))
-
-    for k, buf in enumerate((sheet_f, sheet_i)):
-        arrived(has_prev, buf.at[:, mid, :], buf.at[:, before, :], sheet_send.at[2 * k], sheet_recv.at[2 * k])
-        arrived(has_next, buf.at[:, mid, :], buf.at[:, after, :], sheet_send.at[2 * k + 1], sheet_recv.at[2 * k + 1])
+    arrived(has_prev, sheet.at[:, mid, :], sheet.at[:, before, :], sheet_send.at[0], sheet_recv.at[0])
+    arrived(has_next, sheet.at[:, mid, :], sheet.at[:, after, :], sheet_send.at[1], sheet_recv.at[1])
 
     def field_steps(n, first_row):
         row_id = lax.broadcasted_iota(jnp.int32, (n, width), 0) + first_row
@@ -250,9 +240,9 @@
 
     def krylov(warm, volt, pattern, first_row, count):
         valid, sides = field_steps(warm.shape[0], first_row)
-        sigma = jnp.where(valid, jnp.where(pattern == 1, copper_factor, 1.0) / (1.0 + sheet_slope * warm), 0.0)
+        sigma = jnp.where(valid, jnp.where(pattern == 1.0, copper_factor, 1.0) / (1.0 + sheet_slope * warm), 0.0)
         coeffs = [0.5 * (sigma + side(sigma)) for side in sides]
-        contact = jnp.where(pattern == 2, contact_gain, 0.0)
+        contact = jnp.where(pattern == 2.0, contact_gain, 0.0)
         diagonal = leak_diag + contact + coeffs[0] + coeffs[1] + coeffs[2] + coeffs[3]
         basis = [jnp.where(valid, contact * volt, 0.0)]
         for _ in range(count - 1):
@@ -303,30 +293,43 @@
         both = [jnp.where(lane < 64, a, b) for a, b in zip(eight, ninth)]
         return jnp.where(is_low, both[1], both[0])
 
-    _, _, basis = krylov(sheet_f[0], sheet_f[1], sheet_i[0], (g - 1) * rs, 4)
+    _, _, basis = krylov(sheet[0], sheet[1], sheet[2], (g - 1) * rs, 4)
     cross_up, cross_down = (s == 0) & (m > 0), (s == S - 1) & (m < M - 1)
     is_cross = cross_up | cross_down
     red1[s] = jnp.where(is_cross, 0.0, gram_tile(basis, rs, 2 * rs))
 
     @pl.when(is_middle)
     def _():
-        for k, (buf, border) in enumerate(((sheet_f, border_f), (sheet_i, border_i))):
-            for slot in range(4):
-                arrived(None, buf.at[:, mid, :], border.at[:, slot * rs : (slot + 1) * rs, :], border_send.at[k], border_recv.at[k, slot])
-
-    for k, (border, cross) in enumerate(((border_f, cross_f), (border_i, cross_i))):
-        remote(is_middle, border.at[:, 2 * rs : 3 * rs, :], cross, pass_send.at[k, 0], pass_recv.at[k], (m, S - 1))
-        remote(is_middle, border.at[:, rs : 2 * rs, :], cross, pass_send.at[k, 1], pass_recv.at[k], (m + 1, 0))
+        for slot in range(4):
+            arrived(None, sheet.at[:, mid, :], border.at[:, slot * rs : (slot + 1) * rs, :], border_send.at[0], border_recv.at[slot])
+
+    remote(is_middle, border.at[:, 2 * rs : 3 * rs, :], cross, pass_send.at[0], pass_recv.at[0], (m, S - 1))
+    remote(is_middle, border.at[:, rs : 2 * rs, :], cross, pass_send.at[1], pass_recv.at[0], (m + 1, 0))
 
     @pl.when(is_middle)
     def _():
-        _, _, fields = krylov(border_f[0], border_f[1], border_i[0], (m * S + S - 2) * rs, 4)
+        _, _, fields = krylov(border[0], border[1], border[2], (m * S + S - 2) * rs, 4)
         tile = gram_tile(fields, rs, 3 * rs)
         red1[s] = packed(pair_add(unpacked(red1[s]), unpacked(tile)))
 
     for d in range(1, S):
         remote(None, red1.at[s], red1.at[s], r1_send.at[d], r1_recv.at[d], (m, lax.rem(s + d, S)))
 
+    arrived(m > 0, layer.at[:, end_rows, :], layer.at[:, top_halo, :], len_send.at[0], len_recv.at[0])
+    arrived(m < M - 1, layer.at[:, top_rows, :], layer.at[:, end_halo, :], len_send.at[1], len_recv.at[1])
+    remote(s < S - 1, layer, first_b.at[0], rad_send.at[0], rad_recv.at[0], (m, s + 1))
+    remote(s > 0, layer, first_b.at[2], rad_send.at[1], rad_recv.at[1], (m, s - 1))
+
+    def pair_of(ref, i):
+        return unpacked(ref[i])
+
+    for d in range(1, S):
+        src = lax.rem(s + S - d, S)
+        arrived(None, red1.at[s], red1.at[src], r1_send.at[d], r1_recv.at[d])
+    total = tree([pair_of(red1, i) for i in range(S)], pair_add)
+    red2[m] = packed(total)
+    for d in range(1, M):
+        remote(None, red2.at[m], red2.at[m], r2_send.at[d], r2_recv.at[d], (lax.rem(m + d, M), s))
     arrived(s > 0, layer, first_b.at[0], rad_send.at[0], rad_recv.at[0])
     arrived(s < S - 1, layer, first_b.at[2], rad_send.at[1], rad_recv.at[1])
 
@@ -354,37 +357,24 @@
         remote(s >= d, part(REACH, d), part(REACH + d, d), late_send.at[2 * d - 1], late_recv.at[2 * d - 1], (m, s - d))
     late, pending = pending, []
 
-    def pair_of(ref, i):
-        return unpacked(ref[i])
-
-    for d in range(1, S):
-        src = lax.rem(s + S - d, S)
-        arrived(None, red1.at[s], red1.at[src], r1_send.at[d], r1_recv.at[d])
-    total = tree([pair_of(red1, i) for i in range(S)], pair_add)
-    red2[m] = packed(total)
-    for d in range(1, M):
-        remote(None, red2.at[m], red2.at[m], r2_send.at[d], r2_recv.at[d], (lax.rem(m + d, M), s))
-    for k, (border, cross) in enumerate(((border_f, cross_f), (border_i, cross_i))):
-        arrived(is_cross, border.at[:, before, :], cross, pass_send.at[k, 0], pass_recv.at[k])
+    arrived(is_cross, border.at[:, before, :], cross, pass_send.at[0], pass_recv.at[0])
 
     @pl.when(cross_up)
     def _():
-        sheet_f[:, before, :] = cross_f[...]
-        sheet_i[:, before, :] = cross_i[...]
+        sheet[:, before, :] = cross[...]
 
     @pl.when(cross_down)
     def _():
-        sheet_f[:, after, :] = cross_f[...]
-        sheet_i[:, after, :] = cross_i[...]
-
-    coeffs, sides, basis = krylov(sheet_f[0], sheet_f[1], sheet_i[0], (g - 1) * rs, 3)
+        sheet[:, after, :] = cross[...]
+
+    coeffs, sides, basis = krylov(sheet[0], sheet[1], sheet[2], (g - 1) * rs, 3)
 
     before_string = s == 0
 
     def outer(a):
         return jnp.where(before_string, pltpu.roll(a[0:rs], 3, 0), a[2 * rs :])
 
-    cell_ext = outer(sheet_i[1]) - base_cell
+    cell_ext = outer(sheet[3]).astype(jnp.int32) - base_cell
     cell_ext = jnp.clip(cell_ext, 0, 2 * spokes - 1)
     upper_ext = cell_ext >= spokes
     col_ext = jnp.where(upper_ext, cell_ext - spokes, cell_ext)
@@ -542,8 +532,8 @@
             in_specs=[pl.BlockSpec(memory_space=pltpu.HBM)] * 6,
             out_specs=[pl.BlockSpec(memory_space=pltpu.VMEM)] * 2,
             scratch_shapes=[
-                pltpu.VMEM((2, 3 * rs, width), F32),
-                pltpu.VMEM((2, 3 * rs, width), jnp.int32),
+                pltpu.VMEM((4, 3 * rs, width), F32),
+                pltpu.VMEM((2, rs, width), jnp.int32),
                 pltpu.VMEM((rows, spokes), jnp.int32),
                 pltpu.VMEM((3, 2, brick, spokes), F32),
                 pltpu.VMEM((2 * REACH + 1, 2, brick, spokes), F32),
@@ -555,14 +545,12 @@
                 pltpu.VMEM((2 * REACH + 2, brick, spokes), F32),
                 pltpu.VMEM((2 * REACH + 1, brick, spokes), F32),
                 pltpu.VMEM((2 * REACH + 1, brick, spokes), F32),
-                pltpu.VMEM((2, 4 * rs, width), F32),
-                pltpu.VMEM((2, 4 * rs, width), jnp.int32),
-                pltpu.VMEM((2, rs, width), F32),
-                pltpu.VMEM((2, rs, width), jnp.int32),
-                dma((2,)), dma((2, 4)),
-                dma((2, 2)), dma((2,)),
+                pltpu.VMEM((4, 4 * rs, width), F32),
+                pltpu.VMEM((4, rs, width), F32),
+                dma((1,)), dma((4,)),
+                dma((2,)), dma((1,)),
                 dma((6,)),
-                dma((4,)), dma((4,)),
+                dma((2,)), dma((2,)),
                 dma((2,)), dma((2,)),
                 dma((2,)), dma((2,)),
                 dma((2 * REACH,)), dma((2 * REACH,)),

time: 23.4 us -> 23.7 us (1.013)
  the two profiles are of different devices: /device:TPU:9 before, /device:TPU:1 now
where the time goes in v5:
time: 23.7 us; the launch traced here: 23.5 us
  Pallas kernels  20.9 us (88%)
  local copies, waits for them, and re-layouts  1.95 us (8%)
  between operations  0.65 us (3%)
    pallas_call x1, Pallas kernels, local(): pl.pallas_call(functools.partial(kernel, M, S, depth * S), out_shape=shap...  20.9 us
    unnamed x4, local copies, waits for them, and re-layouts  1.95 us

profile of v5, /device:TPU:1, one launch (start us, length us, event | category | flops | bytes accessed | tf_op | source)
XLA Modules:
  0.0 23.5 jit_solution(10797639022015496633)
XLA Ops:
  0.6 20.9 %window.1 = (f32[8,512]{1,0:T(8,128)}, f32[1,64,128]{2,1,0:T(8,128)}) custom-call(f32[8,512]{1,0:T(8,128)} %warm_in.1, f32[8,512]{1,0:T(8,128)} %volt_in.1, s32[8,512]{1,0:T(8,128)} %pat_in.1, s32[64,512]{1,0:T(8,128)} %map_in.1, f32[1,64,128]{2,1,0:T(8,128)} %temp_in.1, s32[1,64,128]{2,1,0:T(8,128)} %kind_in.1), custom_call_target="tpu_custom_call" | custom-call | tf_op jit(solution)/shard_map/window/pallas_call | solution.py:529
  21.5 0.0 copy-start
  21.5 1.3 %copy.10 = f32[8,512]{1,0:T(8,128)} copy(f32[8,512]{1,0:T(8,128)} %get-tuple-element.4) | data formatting | bytes 32768
  22.8 0.0 copy-done
  22.8 0.6 %copy.11 = f32[1,64,128]{2,1,0:T(8,128)} copy(f32[1,64,128]{2,1,0:T(8,128)S(1)} %copy-done) | data formatting | bytes 65536
Async XLA Ops:
  21.5 1.3 %copy-start = (f32[1,64,128]{2,1,0:T(8,128)S(1)}, f32[1,64,128]{2,1,0:T(8,128)}, u32[]{:S(2)}) copy-start(f32[1,64,128]{2,1,0:T(8,128)} %get-tuple-element.5) | copy-start | bytes 98308

commit v6 on v5

--- a/solution.py
+++ b/solution.py
@@ -18,6 +18,7 @@
 conduct_table = (0.3, 1.0, 2.0, 0.6)
 capacity_table = (1.0, 1.5, 2.0, 1.2)
 diffusivity_derivative = 0.4
+NEAR = 4
 REACH = 3
 GRAM = ((0, 0), (0, 1), (0, 2), (0, 3), (1, 1), (1, 2), (1, 3), (2, 2), (2, 3))
 
@@ -94,7 +95,7 @@
     sheet, ints, kind_v, first_b, later_b, onehot, red1, red2, heat_own, heat_ext, heat_b, base_b, rate_b,
     border, cross,
     border_send, border_recv, pass_send, pass_recv,
-    local_sem, sheet_send, sheet_recv, len_send, len_recv, rad_send, rad_recv, late_send, late_recv,
+    known_sem, local_sem, sheet_send, sheet_recv, len_send, len_recv, rad_send, rad_recv, late_send, late_recv,
     r1_send, r1_recv, r2_send, r2_recv, h_send, h_recv, e_send, e_recv,
 ):
     m = lax.axis_index("magnet")
@@ -135,8 +136,11 @@
     def greet(who):
         pl.semaphore_signal(barrier, inc=1, device_id=who, device_id_type=MESH)
 
-    for d in range(1, S):
-        greet((m, lax.rem(s + d, S)))
+    count = M - 1
+    for d in range(1, NEAR + 1):
+        pl.when(s >= d)(lambda: greet((m, s - d)))
+        pl.when(s < S - d)(lambda: greet((m, s + d)))
+        count = count + jnp.where(s >= d, 1, 0) + jnp.where(s < S - d, 1, 0)
     for d in range(1, M):
         greet((lax.rem(m + d, M), s))
     middle = S // 2 - 1
@@ -149,12 +153,21 @@
         greet((m + 1, 0))
         greet((m + 1, 1))
 
-    extra = jnp.where(at_top, 1, 0) + jnp.where(is_middle, 2, 0)
+    count = count + jnp.where(at_top, 1, 0) + jnp.where(is_middle, 2, 0)
+    if S - 1 - middle > NEAR:
+        pl.when(at_end)(lambda: greet((m, middle)))
+
+        @pl.when(is_middle)
+        def _():
+            greet((m, S - 2))
+            greet((m, S - 1))
+
+        count = count + jnp.where(at_end, 1, 0) + jnp.where(is_middle, 2, 0)
     for c in local:
         c.wait()
     sheet[2:4, rs : 2 * rs, :] = ints[...].astype(F32)
     first_b[1, 1, bmid, :] = kind_v[...].astype(F32)
-    pl.semaphore_wait(barrier, S + M - 2 + extra)
+    pl.semaphore_wait(barrier, count)
 
     pending = []
 
@@ -217,6 +230,24 @@
 
     arrived(has_prev, sheet.at[:, mid, :], sheet.at[:, before, :], sheet_send.at[0], sheet_recv.at[0])
     arrived(has_next, sheet.at[:, mid, :], sheet.at[:, after, :], sheet_send.at[1], sheet_recv.at[1])
+
+    hops, known = [], NEAR + 1
+    while known < S - 1:
+        hops.append(min(known, S - 1 - known))
+        known += hops[-1]
+
+    def tell(n, d):
+        def signal(who):
+            pl.semaphore_signal(known_sem.at[n], inc=1, device_id=who, device_id_type=MESH)
+
+        pl.when(s >= d)(lambda: signal((m, s - d)))
+        pl.when(s < S - d)(lambda: signal((m, s + d)))
+
+    def hear(n, d):
+        pl.semaphore_wait(known_sem.at[n], jnp.where(s >= d, 1, 0) + jnp.where(s < S - d, 1, 0))
+
+    if hops:
+        tell(0, hops[0])
 
     def field_steps(n, first_row):
         row_id = lax.broadcasted_iota(jnp.int32, (n, width), 0) + first_row
@@ -298,6 +329,11 @@
     is_cross = cross_up | cross_down
     red1[s] = jnp.where(is_cross, 0.0, gram_tile(basis, rs, 2 * rs))
 
+    arrived(m > 0, layer.at[:, end_rows, :], layer.at[:, top_halo, :], len_send.at[0], len_recv.at[0])
+    arrived(m < M - 1, layer.at[:, top_rows, :], layer.at[:, end_halo, :], len_send.at[1], len_recv.at[1])
+    remote(s < S - 1, layer, first_b.at[0], rad_send.at[0], rad_recv.at[0], (m, s + 1))
+    remote(s > 0, layer, first_b.at[2], rad_send.at[1], rad_recv.at[1], (m, s - 1))
+
     @pl.when(is_middle)
     def _():
         for slot in range(4):
@@ -312,24 +348,13 @@
         tile = gram_tile(fields, rs, 3 * rs)
         red1[s] = packed(pair_add(unpacked(red1[s]), unpacked(tile)))
 
+    for n, d in enumerate(hops):
+        if n:
+            tell(n, d)
+        hear(n, d)
     for d in range(1, S):
         remote(None, red1.at[s], red1.at[s], r1_send.at[d], r1_recv.at[d], (m, lax.rem(s + d, S)))
 
-    arrived(m > 0, layer.at[:, end_rows, :], layer.at[:, top_halo, :], len_send.at[0], len_recv.at[0])
-    arrived(m < M - 1, layer.at[:, top_rows, :], layer.at[:, end_halo, :], len_send.at[1], len_recv.at[1])
-    remote(s < S - 1, layer, first_b.at[0], rad_send.at[0], rad_recv.at[0], (m, s + 1))
-    remote(s > 0, layer, first_b.at[2], rad_send.at[1], rad_recv.at[1], (m, s - 1))
-
-    def pair_of(ref, i):
-        return unpacked(ref[i])
-
-    for d in range(1, S):
-        src = lax.rem(s + S - d, S)
-        arrived(None, red1.at[s], red1.at[src], r1_send.at[d], r1_recv.at[d])
-    total = tree([pair_of(red1, i) for i in range(S)], pair_add)
-    red2[m] = packed(total)
-    for d in range(1, M):
-        remote(None, red2.at[m], red2.at[m], r2_send.at[d], r2_recv.at[d], (lax.rem(m + d, M), s))
     arrived(s > 0, layer, first_b.at[0], rad_send.at[0], rad_recv.at[0])
     arrived(s < S - 1, layer, first_b.at[2], rad_send.at[1], rad_recv.at[1])
 
@@ -357,6 +382,16 @@
         remote(s >= d, part(REACH, d), part(REACH + d, d), late_send.at[2 * d - 1], late_recv.at[2 * d - 1], (m, s - d))
     late, pending = pending, []
 
+    def pair_of(ref, i):
+        return unpacked(ref[i])
+
+    for d in range(1, S):
+        src = lax.rem(s + S - d, S)
+        arrived(None, red1.at[s], red1.at[src], r1_send.at[d], r1_recv.at[d])
+    total = tree([pair_of(red1, i) for i in range(S)], pair_add)
+    red2[m] = packed(total)
+    for d in range(1, M):
+        remote(None, red2.at[m], red2.at[m], r2_send.at[d], r2_recv.at[d], (lax.rem(m + d, M), s))
     arrived(is_cross, border.at[:, before, :], cross, pass_send.at[0], pass_recv.at[0])
 
     @pl.when(cross_up)
@@ -549,6 +584,7 @@
                 pltpu.VMEM((4, rs, width), F32),
                 dma((1,)), dma((4,)),
                 dma((2,)), dma((1,)),
+                pltpu.SemaphoreType.REGULAR((8,)),
                 dma((6,)),
                 dma((2,)), dma((2,)),
                 dma((2,)), dma((2,)),

time: 23.7 us -> 23.7 us (level)
  the two profiles are of different devices: /device:TPU:1 before, /device:TPU:0 now
where the time goes in v6:
time: 23.7 us; the launch traced here: 23.5 us
  Pallas kernels  20.9 us (88%)
  local copies, waits for them, and re-layouts  1.95 us (8%)
  between operations  0.65 us (3%)
    pallas_call x1, Pallas kernels, local(): pl.pallas_call(functools.partial(kernel, M, S, depth * S), out_shape=shap...  20.9 us
    unnamed x4, local copies, waits for them, and re-layouts  1.95 us

profile of v6, /device:TPU:0, one launch (start us, length us, event | category | flops | bytes accessed | tf_op | source)
XLA Modules:
  0.0 23.5 jit_solution(14789992361732537393)
XLA Ops:
  0.6 20.9 %window.1 = (f32[8,512]{1,0:T(8,128)}, f32[1,64,128]{2,1,0:T(8,128)}) custom-call(f32[8,512]{1,0:T(8,128)} %warm_in.1, f32[8,512]{1,0:T(8,128)} %volt_in.1, s32[8,512]{1,0:T(8,128)} %pat_in.1, s32[64,512]{1,0:T(8,128)} %map_in.1, f32[1,64,128]{2,1,0:T(8,128)} %temp_in.1, s32[1,64,128]{2,1,0:T(8,128)} %kind_in.1), custom_call_target="tpu_custom_call" | custom-call | tf_op jit(solution)/shard_map/window/pallas_call | solution.py:564
  21.5 0.0 copy-start
  21.5 1.3 %copy.10 = f32[8,512]{1,0:T(8,128)} copy(f32[8,512]{1,0:T(8,128)} %get-tuple-element.4) | data formatting | bytes 32768
  22.9 0.0 copy-done
  22.9 0.6 %copy.11 = f32[1,64,128]{2,1,0:T(8,128)} copy(f32[1,64,128]{2,1,0:T(8,128)S(1)} %copy-done) | data formatting | bytes 65536
Async XLA Ops:
  21.5 1.3 %copy-start = (f32[1,64,128]{2,1,0:T(8,128)S(1)}, f32[1,64,128]{2,1,0:T(8,128)}, u32[]{:S(2)}) copy-start(f32[1,64,128]{2,1,0:T(8,128)} %get-tuple-element.5) | copy-start | bytes 98308

commit v7 on v4

--- a/solution.py
+++ b/solution.py
@@ -523,6 +523,11 @@
     sent(pending)
 
 
+def hand_over(pot, brick, pot_out, brick_out):
+    pot_out[...] = pot[...]
+    brick_out[...] = brick[...]
+
+
 def solution(mesh):
     M, S = mesh.shape["magnet"], mesh.shape["slab"]
 
@@ -536,7 +541,7 @@
             jax.ShapeDtypeStruct((rs, width), F32),
             jax.ShapeDtypeStruct((depth, rows, spokes), F32),
         )
-        return pl.pallas_call(
+        outs = pl.pallas_call(
             functools.partial(kernel, M, S, depth * S),
             out_shape=shapes,
             in_specs=[pl.BlockSpec(memory_space=pltpu.HBM)] * 6,
@@ -576,6 +581,14 @@
             ),
             name="window",
         )(warm, volt, pattern, cells, temp, kind)
+        return pl.pallas_call(
+            hand_over,
+            out_shape=shapes,
+            in_specs=[pl.BlockSpec(memory_space=pltpu.VMEM)] * 2,
+            out_specs=[pl.BlockSpec(memory_space=pltpu.VMEM)] * 2,
+            compiler_params=pltpu.CompilerParams(vmem_limit_bytes=63 * 1024 * 1024),
+            name="hand_over",
+        )(*outs)
 
     return jax.shard_map(
         local,

time: 23.4 us -> 22.9 us (0.979)
  local copies, waits for them, and re-layouts: 1.95 us -> 0 us
  Pallas kernels: 20.5 us -> 21.9 us
    unnamed x4 -> x0, local copies, waits for them, and re-layouts: 1.95 us -> none
    pallas_call x0 -> x1, Pallas kernels: none -> 1.4 us  [local(): pl.pallas_call(hand_over, out_shape=shapes, in_specs=[pl.BlockSpec(memory...]
where the time goes in v7:
time: 22.9 us; the launch traced here: 22.6 us
  Pallas kernels  21.9 us (96%)
  between operations  0.64 us (3%)
    pallas_call x1, Pallas kernels, local(): pl.pallas_call(functools.partial(kernel, M, S, depth * S), out_shape=shap...  20.6 us
    pallas_call x1, Pallas kernels, local(): pl.pallas_call(hand_over, out_shape=shapes, in_specs=[pl.BlockSpec(memory...  1.4 us

profile of v7, /device:TPU:9, one launch (start us, length us, event | category | flops | bytes accessed | tf_op | source)
XLA Modules:
  0.0 22.6 jit_solution(8523112453236800913)
XLA Ops:
  0.6 20.6 %window.1 = (f32[8,512]{1,0:T(8,128)}, f32[1,64,128]{2,1,0:T(8,128)}) custom-call(f32[8,512]{1,0:T(8,128)} %warm_in.1, f32[8,512]{1,0:T(8,128)} %volt_in.1, s32[8,512]{1,0:T(8,128)} %pat_in.1, s32[64,512]{1,0:T(8,128)} %map_in.1, f32[1,64,128]{2,1,0:T(8,128)} %temp_in.1, s32[1,64,128]{2,1,0:T(8,128)} %kind_in.1), custom_call_target="tpu_custom_call" | custom-call | tf_op jit(solution)/shard_map/window/pallas_call | solution.py:544
  21.2 1.4 %hand_over.1 = (f32[8,512]{1,0:T(8,128)}, f32[1,64,128]{2,1,0:T(8,128)}) custom-call(f32[8,512]{1,0:T(8,128)} %get-tuple-element.4.pot, f32[1,64,128]{2,1,0:T(8,128)} %get-tuple-element.5.brick), custom_call_target="tpu_custom_call" | custom-call | tf_op jit(solution)/shard_map/hand_over/pallas_call | solution.py:584

commit v8 on v7

--- a/solution.py
+++ b/solution.py
@@ -473,7 +473,7 @@
         return pl.ds(REACH + S - 2 - t, 2)
 
     mine, pending = pending, []
-    for n, t in enumerate(range(target0, S)):
+    for n, t in enumerate(reversed(range(target0, S))):
         remote(s != t, heat_own, heat_b.at[slots(t), at, :], h_send.at[n], h_recv.at[s], (m, t))
     ext_lower, ext_higher = binned(outer(joule), upper_ext, rs, 3)
     heat_ext[0] = jnp.where(before_string, pltpu.roll(ext_lower, rs - 3, 0), ext_lower)
@@ -481,7 +481,7 @@
     at_rim = (s == 0) | (s == S - 1)
     side_of = jnp.where(before_string, 0, 1)
     ext_at = pl.ds(pl.multiple_of(jnp.where(before_string, 0, rows + 8), 8), 8)
-    for n, t in enumerate(range(target0, S)):
+    for n, t in enumerate(reversed(range(target0, S))):
         remote(at_rim & (s != t), heat_ext, heat_b.at[slots(t), ext_at, :], e_send.at[n], e_recv.at[side_of], (m, t))
 
     @pl.when(heated)

time: 22.9 us -> 23.1 us (level)
  no operation moved by 1% of the time
where the time goes in v8:
time: 23.1 us; the launch traced here: 22.8 us
  Pallas kernels  22.1 us (96%)
  between operations  0.64 us (3%)
    pallas_call x1, Pallas kernels, local(): pl.pallas_call(functools.partial(kernel, M, S, depth * S), out_shape=shap...  20.7 us
    pallas_call x1, Pallas kernels, local(): pl.pallas_call(hand_over, out_shape=shapes, in_specs=[pl.BlockSpec(memory...  1.4 us

profile of v8, /device:TPU:9, one launch (start us, length us, event | category | flops | bytes accessed | tf_op | source)
XLA Modules:
  0.0 22.8 jit_solution(12631808842715359778)
XLA Ops:
  0.6 20.7 %window.1 = (f32[8,512]{1,0:T(8,128)}, f32[1,64,128]{2,1,0:T(8,128)}) custom-call(f32[8,512]{1,0:T(8,128)} %warm_in.1, f32[8,512]{1,0:T(8,128)} %volt_in.1, s32[8,512]{1,0:T(8,128)} %pat_in.1, s32[64,512]{1,0:T(8,128)} %map_in.1, f32[1,64,128]{2,1,0:T(8,128)} %temp_in.1, s32[1,64,128]{2,1,0:T(8,128)} %kind_in.1), custom_call_target="tpu_custom_call" | custom-call | tf_op jit(solution)/shard_map/window/pallas_call | solution.py:544
  21.4 1.4 %hand_over.1 = (f32[8,512]{1,0:T(8,128)}, f32[1,64,128]{2,1,0:T(8,128)}) custom-call(f32[8,512]{1,0:T(8,128)} %get-tuple-element.4.pot, f32[1,64,128]{2,1,0:T(8,128)} %get-tuple-element.5.brick), custom_call_target="tpu_custom_call" | custom-call | tf_op jit(solution)/shard_map/hand_over/pallas_call | solution.py:584
